TPU v7x, 128 devices: a whole 4x4x4 slice. The times are simulated.
128 devices in a mesh: rows: 16 (over z, y), cols: 8 (over x, core).
Axes of the slice: x: 4, y: 4, z: 4, core: 2. Of those that a mesh axis runs over, the one named last changes fastest.
Arguments:
- history: bfloat16 [384, 128, 1024], P(('rows', 'cols')), may hold values from -24 to 24
- qkv_weight: bfloat16 [1024, 3072], replicated, may hold values from -0.1875 to 0.1875
- out_weight: bfloat16 [1024, 1024], replicated, may hold values from -0.1875 to 0.1875
- pool_weight: bfloat16 [1024, 1024], replicated, may hold values from -0.1875 to 0.1875
- head_weight: bfloat16 [1024, 1024], replicated, may hold values from -0.1875 to 0.1875
- risk_weight: float32 [1024], replicated, may hold values from -0.1875 to 0.1875
- time_table: float32 [128, 1024], replicated, may hold values from -3 to 3
- case_rows: int32 [384], P(('rows', 'cols')), may hold values from 0 to 2, as said below
- control_rows: int32 [384, 32], P(('rows', 'cols')), may hold values from 0 to 383, as said below
- buckets: int32 [384], P(('rows', 'cols')), may hold values from 0 to 127
- case_weight: float32 [384], P(('rows', 'cols')), may hold values from 8 to 64
Outputs:
- grad_input: float32 [384, 128, 1024], P(('rows', 'cols'))
- grad_qkv: float32 [1024, 3072], P(('rows', 'cols'))
- grad_out: float32 [1024, 1024], P(('rows', 'cols'))
- grad_pool: float32 [1024, 1024], P(('rows', 'cols'))
- grad_head: float32 [1024, 1024], P(('rows', 'cols'))
Inputs may be any that keep to these rules, and one draw needn't show every extreme that they name: `case_rows`: the 3 cases of one device name distinct histories of that device, counted from 0. `control_rows`: history r lies on the device at place r // 3 along rows+cols. Among the controls of one device's cases, at most 4 lie on any one device, and for every device's cases some device holds exactly 4 of them.
All inputs are finite; a program needn't handle non-finite values.
Results may differ from a plain program's by a relative error of at most 0.015.
Values may be sent and summed in bfloat16 or wider, within the bound.
A program may use at most 128 MiB of HBM per device.

v0:
```python
import math

import jax
import jax.numpy as jnp
from jax import lax
from jax.sharding import PartitionSpec as P

D = 1024
HD = 64
HEADS = 16
S = 128
K = 32
CAP = 4
NB = 128
R_DEV = 3
C_DEV = 3


def encode(history, qkv_weight, out_weight, pool_weight):
    row_count = history.shape[0]
    widened = history.astype(jnp.float32)
    inverse = lax.rsqrt(jnp.mean(widened * widened, axis=-1, keepdims=True) + 1e-05)
    normed = (widened * inverse).astype(jnp.bfloat16).reshape(row_count * S, D)
    packed = jnp.dot(normed, qkv_weight, preferred_element_type=jnp.float32).astype(jnp.bfloat16)
    packed = packed.reshape(row_count, S, 3, HEADS, HD)
    query_part = packed[:, :, 0]
    key_part = packed[:, :, 1]
    value_part = packed[:, :, 2]
    logits = jnp.einsum(
        "rshd,rthd->rhst", query_part, key_part, preferred_element_type=jnp.float32
    ) / math.sqrt(HD)
    raised = jnp.exp(logits)
    attention = raised / jnp.sum(raised, axis=-1, keepdims=True)
    attention_low = attention.astype(jnp.bfloat16)
    mixture = jnp.einsum(
        "rhst,rthd->rshd", attention_low, value_part, preferred_element_type=jnp.float32
    )
    mixture = mixture.astype(jnp.bfloat16).reshape(row_count * S, D)
    residual = widened.reshape(row_count * S, D) + jnp.dot(
        mixture, out_weight, preferred_element_type=jnp.float32
    )
    residual_low = residual.astype(jnp.bfloat16)
    active = jnp.tanh(jnp.dot(residual_low, pool_weight, preferred_element_type=jnp.float32))
    pooled = (jnp.sum(active.reshape(row_count, S, D), axis=1) / math.sqrt(S)).astype(jnp.bfloat16)
    stored = (
        widened,
        inverse,
        normed,
        query_part,
        key_part,
        value_part,
        attention,
        attention_low,
        mixture,
        residual_low,
        active,
    )
    return (pooled, stored)


def backward(stored, grad_pooled, qkv_weight, out_weight, pool_weight):
    (
        widened,
        inverse,
        normed,
        query_part,
        key_part,
        value_part,
        attention,
        attention_low,
        mixture,
        residual_low,
        active,
    ) = stored
    row_count = grad_pooled.shape[0]
    grad_active = jnp.broadcast_to(
        grad_pooled[:, None, :] / math.sqrt(S), (row_count, S, D)
    ).reshape(row_count * S, D)
    grad_pre = (grad_active * (1.0 - active * active)).astype(jnp.bfloat16)
    pool_grad = jnp.einsum("nd,ne->de", residual_low, grad_pre, preferred_element_type=jnp.float32)
    grad_residual = jnp.einsum(
        "ne,de->nd", grad_pre, pool_weight, preferred_element_type=jnp.float32
    )
    grad_residual_low = grad_residual.astype(jnp.bfloat16)
    out_grad = jnp.einsum(
        "nd,ne->de", mixture, grad_residual_low, preferred_element_type=jnp.float32
    )
    grad_mixture = jnp.einsum(
        "ne,de->nd", grad_residual_low, out_weight, preferred_element_type=jnp.float32
    )
    grad_mixture = grad_mixture.astype(jnp.bfloat16).reshape(row_count, S, HEADS, HD)
    grad_attention = jnp.einsum(
        "rshd,rthd->rhst", grad_mixture, value_part, preferred_element_type=jnp.float32
    )
    grad_values = jnp.einsum(
        "rhst,rshd->rthd", attention_low, grad_mixture, preferred_element_type=jnp.float32
    )
    grad_logits = (
        attention
        * (grad_attention - jnp.sum(attention * grad_attention, axis=-1, keepdims=True))
        / math.sqrt(HD)
    )
    grad_logits = grad_logits.astype(jnp.bfloat16)
    grad_query = jnp.einsum(
        "rhst,rthd->rshd", grad_logits, key_part, preferred_element_type=jnp.float32
    )
    grad_keys = jnp.einsum(
        "rhst,rshd->rthd", grad_logits, query_part, preferred_element_type=jnp.float32
    )
    grad_packed = (
        jnp.stack([grad_query, grad_keys, grad_values], axis=2)
        .astype(jnp.bfloat16)
        .reshape(row_count * S, 3 * D)
    )
    qkv_grad = jnp.einsum("nd,ne->de", normed, grad_packed, preferred_element_type=jnp.float32)
    grad_normed = jnp.einsum(
        "ne,de->nd", grad_packed, qkv_weight, preferred_element_type=jnp.float32
    ).reshape(row_count, S, D)
    grad_input = grad_residual.reshape(row_count, S, D) + inverse * grad_normed
    grad_input = grad_input - widened * inverse**3 * jnp.mean(
        grad_normed * widened, axis=-1, keepdims=True
    )
    return (grad_input, qkv_grad, out_grad, pool_grad)


def score_cases(member_pooled, time_rows, case_weight, head_weight, risk_weight):
    cases = member_pooled.shape[0]
    hidden = (
        (member_pooled.astype(jnp.float32) + time_rows[:, None, :])
        .astype(jnp.bfloat16)
        .reshape(cases * (K + 1), D)
    )
    preact = jnp.dot(hidden, head_weight, preferred_element_type=jnp.float32)
    gated = jax.nn.sigmoid(preact)
    risk_score = jnp.sum(preact * gated * risk_weight[None, :], axis=-1).reshape(cases, K + 1)
    raised = jnp.exp(risk_score)
    shares = raised / jnp.sum(raised, axis=-1, keepdims=True)
    is_case = (jnp.arange(K + 1) == 0).astype(jnp.float32)
    grad_risk = case_weight[:, None] * (shares - is_case[None, :])
    grad_preact = (
        grad_risk.reshape(cases * (K + 1), 1)
        * risk_weight[None, :]
        * gated
        * (1.0 + preact * (1.0 - gated))
    )
    grad_preact = grad_preact.astype(jnp.bfloat16)
    head_grad = jnp.einsum("nd,ne->de", hidden, grad_preact, preferred_element_type=jnp.float32)
    grad_hidden = jnp.einsum(
        "ne,de->nd", grad_preact, head_weight, preferred_element_type=jnp.float32
    )
    return (grad_hidden.reshape(cases, K + 1, D), head_grad)


def body(
    history,
    qkv_weight,
    out_weight,
    pool_weight,
    head_weight,
    risk_weight,
    time_table,
    case_rows,
    control_rows,
    buckets,
    case_weight,
):
    outer = lax.axis_size("rows")
    inner_size = lax.axis_size("cols")
    groups = outer * inner_size
    pooled, stored = encode(history, qkv_weight, out_weight, pool_weight)
    case_onehot = (case_rows[:, None] == jnp.arange(R_DEV, dtype=jnp.int32)[None, :]).astype(
        jnp.float32
    )
    case_pooled = jnp.take(pooled, case_rows, axis=0)
    flat_rows = control_rows.reshape(C_DEV * K)
    owners = flat_rows // R_DEV
    local_row = flat_rows % R_DEV
    owner_hits = (owners[:, None] == jnp.arange(groups, dtype=jnp.int32)[None, :]).astype(jnp.int32)
    slot_index = jnp.sum((jnp.cumsum(owner_hits, axis=0) - owner_hits) * owner_hits, axis=1)
    position = owners * CAP + slot_index
    requests = jnp.full((groups * CAP,), -1, jnp.int32).at[position].set(local_row)
    asked_rows = lax.all_to_all(
        requests.reshape(groups, CAP), ("rows", "cols"), split_axis=0, concat_axis=0, tiled=True
    )
    picked = jnp.take(pooled, jnp.clip(asked_rows, 0, R_DEV - 1), axis=0)
    replies = lax.all_to_all(picked, ("rows", "cols"), split_axis=0, concat_axis=0, tiled=True)
    control_pooled = jnp.take(replies.reshape(groups * CAP, D), position, axis=0)
    member_pooled = jnp.concatenate(
        [case_pooled[:, None, :], control_pooled.reshape(C_DEV, K, D)], axis=1
    )
    bucket_onehot = (buckets[:, None] == jnp.arange(NB, dtype=jnp.int32)[None, :]).astype(
        jnp.float32
    )
    time_rows = jnp.dot(bucket_onehot, time_table, precision=lax.Precision.HIGHEST)
    grad_hidden, head_grad = score_cases(
        member_pooled, time_rows, case_weight, head_weight, risk_weight
    )
    case_grad = grad_hidden[:, 0]
    control_grad = grad_hidden[:, 1:].reshape(C_DEV * K, D)
    own_part = jnp.einsum("cr,cd->rd", case_onehot, case_grad, precision=lax.Precision.HIGHEST)
    buffer = jnp.zeros((groups * CAP, D), jnp.float32).at[position].set(control_grad)
    returned = lax.all_to_all(
        buffer.reshape(groups, CAP, D).astype(jnp.bfloat16),
        ("rows", "cols"),
        split_axis=0,
        concat_axis=0,
        tiled=True,
    ).astype(jnp.float32)
    request_hits = (
        asked_rows.reshape(groups * CAP)[:, None] == jnp.arange(R_DEV, dtype=jnp.int32)[None, :]
    ).astype(jnp.float32)
    grad_pooled = (
        jnp.einsum(
            "pr,pd->rd",
            request_hits,
            returned.reshape(groups * CAP, D),
            precision=lax.Precision.HIGHEST,
        )
        + own_part
    )
    grad_input, qkv_grad, out_grad, pool_grad = backward(
        stored, grad_pooled, qkv_weight, out_weight, pool_weight
    )
    shares = (
        lax.psum_scatter(qkv_grad, ("rows", "cols"), scatter_dimension=0, tiled=True),
        lax.psum_scatter(out_grad, ("rows", "cols"), scatter_dimension=0, tiled=True),
        lax.psum_scatter(pool_grad, ("rows", "cols"), scatter_dimension=0, tiled=True),
        lax.psum_scatter(head_grad, ("rows", "cols"), scatter_dimension=0, tiled=True),
    )
    return (grad_input, shares[0], shares[1], shares[2], shares[3])


def solution(mesh):
    in_specs = (
        P(("rows", "cols"), None, None),
        P(),
        P(),
        P(),
        P(),
        P(),
        P(),
        P(("rows", "cols")),
        P(("rows", "cols"), None),
        P(("rows", "cols")),
        P(("rows", "cols")),
    )
    out_specs = (
        P(("rows", "cols"), None, None),
        P(("rows", "cols"), None),
        P(("rows", "cols"), None),
        P(("rows", "cols"), None),
        P(("rows", "cols"), None),
    )
    return jax.shard_map(body, mesh=mesh, in_specs=in_specs, out_specs=out_specs, check_vma=False)
```

profile of v0, /device:TPU:0, one launch (start us, length us, event | category | flops | bytes accessed | tf_op | source)
XLA Modules:
  0.0 2266.0 jit_solution(13948310441353933016)
XLA Ops:
  12.0 11.1 all-to-all-start
  26.8 6.6 convolution_convert_fusion
  33.4 6.7 reshape.349
  40.2 4.9 fusion.75
  45.1 2.0 copy.70
  47.1 2.9 copy.69
  50.0 2.6 copy.71
  52.6 2.0 fusion.5
  58.7 2.1 convolution_tanh_fusion
  60.9 1.5 reduce_sum.80
  63.2 1.5 fusion.76
  64.8 2.8 gather_fusion.1
  67.6 2.2 reshape.315
  69.9 2.8 broadcast_select_fusion
  72.7 10.3 all-to-all-start.1
  85.1 16.6 all-to-all-done.1
  101.7 2.1 reshape.299
  103.8 2.3 gather_fusion.2
  106.3 2.9 multiply_reduce_fusion.3
  109.7 3.8 fusion.67
  113.5 3.4 fusion.68
  116.9 1.8 reshape.300
  119.8 2.3 scatter_custom_fusion.1
  122.1 2.7 convert_element_type.102
  124.9 2.3 convert_element_type.103
  127.1 5.8 all-to-all-start.2
  134.0 18.0 all-to-all-done.2
  152.0 2.1 reshape.302
  154.1 1.7 fusion.48
  156.1 1.6 fusion.17
  158.6 3.2 fusion.78
  161.9 2.2 fusion.77
  165.3 3.2 fusion.31
  170.0 3.5 convolution_convert_fusion.2
  173.5 2.6 reshape.350
  176.1 1.8 copy.51
  177.9 3.5 fusion.39
  181.4 7.4 fusion.21
  188.8 7.3 fusion.24
  196.2 3.2 convolution_bitcast_fusion
  199.7 2.3 copy.58
  202.0 6.6 fusion.8
  209.1 5.1 multiply_reduce_fusion.1
  214.3 1.6 multiply_subtract_fusion
  215.9 540.1 %reduce-scatter.11.cloned.1.call-done = f32[8,1024]{1,0:T(8,128)} async-done(((f32[1024,1024]{1,0:T(8,128)}), f32[8,1024]{1,0:T(8,128)}) %reduce-scatter.11.cloned.1.call-update) | async-done | bytes 32784 | tf_op jit(solution)/shard_map/reduce_scatter | solution.py:228
  756.0 641.1 %reduce-scatter.9.cloned.1.call-done = f32[8,1024]{1,0:T(8,128)} async-done(((f32[1024,1024]{1,0:T(8,128)}), f32[8,1024]{1,0:T(8,128)}) %reduce-scatter.9.cloned.1.call-update) | async-done | bytes 32784 | tf_op jit(solution)/shard_map/reduce_scatter | solution.py:227
  1397.0 640.9 %reduce-scatter.7.cloned.1.call-done = f32[8,1024]{1,0:T(8,128)} async-done(((f32[1024,1024]{1,0:T(8,128)}), f32[8,1024]{1,0:T(8,128)}) %reduce-scatter.7.cloned.1.call-update) | async-done | bytes 32784 | tf_op jit(solution)/shard_map/reduce_scatter | solution.py:226
  2038.0 221.5 %reduce-scatter.5.cloned.1.call-done = f32[8,3072]{1,0:T(8,128)} async-done(((f32[1024,3072]{1,0:T(8,128)}), f32[8,3072]{1,0:T(8,128)}) %reduce-scatter.5.cloned.1.call-update) | async-done | bytes 98320 | tf_op jit(solution)/shard_map/reduce_scatter | solution.py:225
  (126 shorter events, 22.7 us)
Async XLA Ops:
  7.2 51.5 %copy-start = (bf16[1024,1024]{1,0:T(8,128)(2,1)S(1)}, bf16[1024,1024]{1,0:T(8,128)(2,1)}, u32[]{:S(2)}) copy-start(bf16[1024,1024]{1,0:T(8,128)(2,1)} %param.14) | copy-start | bytes 6291460
  12.0 50.7 %all-to-all-start = ((s32[128,1,4]{2,1,0:T(1,128)}), s32[128,1,4]{2,1,0:T(1,128)S(1)}, u32[]{:S(2)}, u32[]{:S(2)}) async-start(s32[128,1,4]{2,1,0:T(1,128)} %bitcast.2), calls=%async_computation | async-start | bytes 131072 | tf_op jit(solution)/shard_map/all_to_all | solution.py:182
  25.8 1.0 copy-start.17
  47.0 5.6 copy-start.11
  52.6 2.1 copy-start.13
  54.7 1.6 copy-start.10
  54.7 1.6 copy-start.24
  54.7 2.3 copy-start.2
  54.7 3.0 copy-start.20
  57.0 3.9 copy-start.3
  58.7 2.2 copy-start.8
  58.7 3.8 copy-start.28
  69.9 13.1 copy-start.29
  69.9 13.9 copy-start.27
  72.7 29.0 %all-to-all-start.1 = ((bf16[128,4,1024]{2,1,0:T(4,128)(2,1)}), bf16[128,4,1024]{2,1,0:T(4,128)(2,1)}, u32[]{:S(2)}, u32[]{:S(2)}) async-start(bf16[128,4,1024]{2,1,0:T(4,128)(2,1)} %broadcast_select_fusion), calls=%async_computation.1 | async-start | bytes 2097152 | tf_op jit(solution)/shard_map/all_to_all | solution.py:186
  83.0 673.0 %reduce-scatter.11.cloned.1.call-start = ((), (), s32[]{:S(2)}) async-start(), calls=%async_computation.10 | async-start | bytes 4227072 | tf_op jit(solution)/shard_map/reduce_scatter | solution.py:228
  85.1 21.3 copy-start.26
  124.9 8.1 copy-start.23
  127.1 24.9 %all-to-all-start.2 = ((bf16[128,4,1024]{2,1,0:T(4,128)(2,1)}), bf16[128,4,1024]{2,1,0:T(4,128)(2,1)}, u32[]{:S(2)}, u32[]{:S(2)}) async-start(bf16[128,4,1024]{2,1,0:T(4,128)(2,1)} %convert_element_type.103), calls=%async_computation.2 | async-start | bytes 2097152 | tf_op jit(solution)/shard_map/all_to_all | solution.py:202
  132.9 1264.2 %reduce-scatter.9.cloned.1.call-start = ((), (), s32[]{:S(2)}) async-start(), calls=%async_computation.9 | async-start | bytes 4227072 | tf_op jit(solution)/shard_map/reduce_scatter | solution.py:227
  154.1 4.5 copy-start.9
  157.8 0.9 copy-start.19
  161.9 1876.1 %reduce-scatter.7.cloned.1.call-start = ((), (), s32[]{:S(2)}) async-start(), calls=%async_computation.8 | async-start | bytes 4227072 | tf_op jit(solution)/shard_map/reduce_scatter | solution.py:226
  161.9 3.4 copy-start.4
  164.2 1.1 copy-start.5
  168.6 1.4 copy-start.6
  168.6 2090.9 %reduce-scatter.5.cloned.1.call-start = ((), (), s32[]{:S(2)}) async-start(), calls=%async_computation.7 | async-start | bytes 12681216 | tf_op jit(solution)/shard_map/reduce_scatter | solution.py:225
  173.5 4.4 copy-start.14
  177.9 3.5 copy-start.15
  177.9 3.5 copy-start.25
  181.4 7.4 copy-start.12
  188.8 7.4 copy-start.16
  196.2 3.2 copy-start.21
  196.2 3.2 copy-start.22
  199.7 2.3 copy-start.18
  209.1 5.2 copy-start.7
  214.3 2045.2 %copy-start.1 = (bf16[1024,1024]{1,0:T(8,128)(2,1)S(1)}, bf16[1024,1024]{1,0:T(8,128)(2,1)}, u32[]{:S(2)}) copy-start(bf16[1024,1024]{1,0:T(8,128)(2,1)} %param.14) | copy-start | bytes 6291460
Sparse Core Ops, SparseCore 0:
  113.6 642.3 reduce-scatter.10
  759.0 637.9 reduce-scatter.8
  1400.0 637.9 reduce-scatter.6
  2044.2 215.2 reduce-scatter.4
where the time goes:
time: 2270 us
  waiting for transfers between devices  2080 us (92%)
  matrix products  71.3 us (3%)
  local copies, waits for them, and re-layouts  56.7 us (2%)
  starting transfers between devices  27.6 us (1%)
    reduce_scatter x1, waiting for transfers between devices, body(): lax.psum_scatter(pool_grad, ('rows', 'cols'), scatter_dimension=0, tiled=...  641 us
    reduce_scatter x1, waiting for transfers between devices, body(): lax.psum_scatter(out_grad, ('rows', 'cols'), scatter_dimension=0, tiled=T...  641 us
    reduce_scatter x1, waiting for transfers between devices, body(): lax.psum_scatter(head_grad, ('rows', 'cols'), scatter_dimension=0, tiled=...  540 us
    reduce_scatter x1, waiting for transfers between devices, body(): lax.psum_scatter(qkv_grad, ('rows', 'cols'), scatter_dimension=0, tiled=T...  222 us
  transfers between devices with their start and end apart: 7, of which 6 were waited for; matrix products, arithmetic and copies ran while one was open for 5% of the time, Pallas kernels for 0%

commit v1 on v0

v1 whole, which is shorter than its diff:
```python
import math

import jax
import jax.numpy as jnp
from jax import lax
from jax.experimental import pallas as pl
from jax.experimental.pallas import tpu as pltpu
from jax.sharding import PartitionSpec as P

D = 1024
HD = 64
HEADS = 16
S = 128
K = 32
CAP = 4
NB = 128
R_DEV = 3
C_DEV = 3
DEVICES = 128
SLOTS = CAP * DEVICES
MEMBERS = SLOTS + 16

MESH = pl.DeviceIdType.MESH
F32 = jnp.float32
BF16 = jnp.bfloat16

WIDE = 512
GROUPS = (
    (0, 0, "zyx"),
    (0, 512, "yxz"),
    (1, 0, "xzy"),
    (1, 512, "zyx"),
    (2, 0, "yxz"),
    (2, 512, "xzy"),
)


def position():
    row = lax.axis_index("rows")
    col = lax.axis_index("cols")
    return {
        "z": lax.div(row, 4),
        "y": lax.rem(row, 4),
        "x": lax.div(col, 2),
        "core": lax.rem(col, 2),
    }


def device_at(place):
    return (place["z"] * 4 + place["y"], place["x"] * 2 + place["core"])


def moved(place, axis, step):
    return {**place, axis: lax.rem(place[axis] + step, 4)}


def remote(source, target, send_sem, recv_sem, place):
    return pltpu.make_async_remote_copy(
        src_ref=source,
        dst_ref=target,
        send_sem=send_sem,
        recv_sem=recv_sem,
        device_id=device_at(place),
        device_id_type=MESH,
    )


def greet(places):
    barrier = pltpu.get_barrier_semaphore()
    for place in places:
        pl.semaphore_signal(barrier, inc=1, device_id=device_at(place), device_id_type=MESH)
    pl.semaphore_wait(barrier, len(places))


def added(*parts):
    total = parts[0].astype(F32)
    for part in parts[1:]:
        total = total + part.astype(F32)
    return total


def grads_kernel(
    normed,
    mixture,
    residual_low,
    hidden,
    grad_packed,
    grad_residual_low,
    grad_pre,
    grad_preact,
    qkv_out,
    out_out,
    pool_out,
    head_out,
    part,
    swap,
    first,
    second_sum,
    second,
    third_sum,
    third,
    swap_send,
    swap_recv,
    first_send,
    first_recv,
    second_send,
    second_recv,
    third_send,
    third_recv,
):
    here = position()
    core = here["core"]
    twin = {**here, "core": 1 - core}
    greet([twin] + [moved(here, axis, step) for axis in "xyz" for step in (1, 2, 3)])

    slabs = (
        ((residual_low, grad_pre, 0, pool_out, 0), (hidden, grad_preact, 0, head_out, 0)),
        ((mixture, grad_residual_low, 0, out_out, 0), (normed, grad_packed, 2048, qkv_out, 2048)),
        ((normed, grad_packed, 0, qkv_out, 0), (normed, grad_packed, 1024, qkv_out, 1024)),
    )
    sends = []

    def send(copy):
        copy.start()
        sends.append(copy)

    def produce(g):
        slab, col0, order = GROUPS[g]

        def step(i, carry):
            z = lax.div(i, 2)
            n = lax.rem(i, 2)
            results = []
            for lhs, rhs, offset, _, _ in slabs[slab]:
                left = lhs[:, pl.ds(pl.multiple_of(z * 256, 256), 256)]
                right = rhs[:, pl.ds(pl.multiple_of(offset + col0 + n * 256, 256), 256)]
                results.append(
                    lax.dot_general(
                        left, right, (((0,), (0,)), ((), ())), preferred_element_type=F32
                    )
                )
            for y in range(4):
                for x in range(4):
                    for c in range(2):
                        row = y * 64 + x * 16 + c * 8
                        block = jnp.concatenate(
                            [r[row : row + 8] for r in results], axis=0
                        ).astype(BF16)
                        digit = {"z": z, "y": y, "x": x}
                        part[
                            g,
                            c,
                            digit[order[0]],
                            digit[order[1]],
                            digit[order[2]],
                            :,
                            pl.ds(pl.multiple_of(n * 256, 256), 256),
                        ] = block
            return carry

        lax.fori_loop(0, 8, step, 0)
        send(
            remote(part.at[g, 1 - core], swap.at[g], swap_send.at[g], swap_recv.at[g], twin)
        )

    def arrived(target, sem):
        remote(target, target, sem, sem, twin).wait_recv()

    def spread(axis, source, landing, send_sems, recv_sems):
        me = here[axis]
        right, left = moved(here, axis, 1), moved(here, axis, 3)
        far = lax.rem(me + 2, 4)
        for slot, digit, half, place in (
            (0, far, 0, right),
            (1, far, 2, left),
            (2, lax.rem(me + 1, 4), 2, right),
            (3, lax.rem(me + 3, 4), 0, left),
        ):
            send(
                remote(
                    source.at[digit, pl.ds(half, 2)],
                    landing.at[slot],
                    send_sems.at[slot],
                    recv_sems.at[slot],
                    place,
                )
            )

    def relay(axis, source, landing, send_sems, recv_sems):
        me = here[axis]
        right, left = moved(here, axis, 1), moved(here, axis, 3)
        for slot, came, digit, half, place in (
            (4, 0, lax.rem(me + 1, 4), 0, right),
            (5, 1, lax.rem(me + 3, 4), 2, left),
        ):
            arrived(landing.at[came], recv_sems.at[came])
            for k in range(2):
                source[digit, half + k] = added(
                    source[digit, half + k], landing[came, k]
                ).astype(BF16)
            send(
                remote(
                    source.at[digit, pl.ds(half, 2)],
                    landing.at[slot],
                    send_sems.at[slot],
                    recv_sems.at[slot],
                    place,
                )
            )

    def collect(axis, source, landing, recv_sems, target):
        me = here[axis]
        for slot in (2, 3, 4, 5):
            arrived(landing.at[slot], recv_sems.at[slot])
        for k in range(2):
            target[k] = added(source[me, k], landing[3, k], landing[4, k]).astype(BF16)
            target[2 + k] = added(source[me, 2 + k], landing[2, k], landing[5, k]).astype(BF16)

    def first_spread(g):
        arrived(swap.at[g], swap_recv.at[g])

        def step(i, carry):
            a = lax.div(i, 4)
            b = lax.rem(i, 4)
            part[g, core, a, b] = added(part[g, core, a, b], swap[g, a, b]).astype(BF16)
            return carry

        lax.fori_loop(0, 16, step, 0)
        spread(GROUPS[g][2][0], part.at[g, core], first.at[g], first_send.at[g], first_recv.at[g])

    def first_relay(g):
        relay(GROUPS[g][2][0], part.at[g, core], first.at[g], first_send.at[g], first_recv.at[g])

    def second_spread(g):
        order = GROUPS[g][2]
        collect(order[0], part.at[g, core], first.at[g], first_recv.at[g], second_sum.at[g])
        spread(order[1], second_sum.at[g], second.at[g], second_send.at[g], second_recv.at[g])

    def second_relay(g):
        relay(
            GROUPS[g][2][1], second_sum.at[g], second.at[g], second_send.at[g], second_recv.at[g]
        )

    def third_spread(g):
        order = GROUPS[g][2]
        collect(order[1], second_sum.at[g], second.at[g], second_recv.at[g], third_sum.at[g])
        axis = order[2]
        for step in (1, 2, 3):
            send(
                remote(
                    third_sum.at[g, lax.rem(here[axis] + step, 4)],
                    third.at[g, step - 1],
                    third_send.at[g, step - 1],
                    third_recv.at[g, step - 1],
                    moved(here, axis, step),
                )
            )

    def finish(g):
        slab, col0, order = GROUPS[g]
        for slot in range(3):
            arrived(third.at[g, slot], third_recv.at[g, slot])
        total = added(third_sum[g, here[order[2]]], third[g, 0], third[g, 1], third[g, 2])
        for t, (_, _, _, out, offset) in enumerate(slabs[slab]):
            out[:, offset + col0 : offset + col0 + WIDE] = total[8 * t : 8 * t + 8]

    stages = (
        produce,
        first_spread,
        first_relay,
        second_spread,
        second_relay,
        third_spread,
        finish,
    )
    for tick in range(len(GROUPS) + len(stages) - 1):
        for s, stage in enumerate(stages):
            if 0 <= tick - s < len(GROUPS):
                stage(tick - s)
    for copy in sends:
        copy.wait_send()


def weight_grads(
    normed, mixture, residual_low, hidden, grad_packed, grad_residual_low, grad_pre, grad_preact
):
    count = len(GROUPS)
    vmem = pl.BlockSpec(memory_space=pltpu.VMEM)
    return pl.pallas_call(
        grads_kernel,
        out_shape=(
            jax.ShapeDtypeStruct((8, 3 * D), F32),
            jax.ShapeDtypeStruct((8, D), F32),
            jax.ShapeDtypeStruct((8, D), F32),
            jax.ShapeDtypeStruct((8, D), F32),
        ),
        in_specs=[vmem] * 8,
        out_specs=(vmem,) * 4,
        scratch_shapes=[
            pltpu.VMEM((count, 2, 4, 4, 4, 16, WIDE), BF16),
            pltpu.VMEM((count, 4, 4, 4, 16, WIDE), BF16),
            pltpu.VMEM((count, 6, 2, 4, 16, WIDE), BF16),
            pltpu.VMEM((count, 4, 4, 16, WIDE), BF16),
            pltpu.VMEM((count, 6, 2, 16, WIDE), BF16),
            pltpu.VMEM((count, 4, 16, WIDE), BF16),
            pltpu.VMEM((count, 3, 16, WIDE), BF16),
            pltpu.SemaphoreType.DMA((count,)),
            pltpu.SemaphoreType.DMA((count,)),
            pltpu.SemaphoreType.DMA((count, 6)),
            pltpu.SemaphoreType.DMA((count, 6)),
            pltpu.SemaphoreType.DMA((count, 6)),
            pltpu.SemaphoreType.DMA((count, 6)),
            pltpu.SemaphoreType.DMA((count, 3)),
            pltpu.SemaphoreType.DMA((count, 3)),
        ],
        compiler_params=pltpu.CompilerParams(
            collective_id=1, has_side_effects=True, vmem_limit_bytes=52 * 2**20
        ),
    )(normed, mixture, residual_low, hidden, grad_packed, grad_residual_low, grad_pre, grad_preact)


def total_kernel(
    own, out, by_row, middle, by_col, row_send, row_recv, col_send, col_recv
):
    row = lax.axis_index("rows")
    col = lax.axis_index("cols")
    barrier = pltpu.get_barrier_semaphore()
    for step in range(1, 16):
        pl.semaphore_signal(
            barrier, inc=1, device_id=(lax.rem(row + step, 16), col), device_id_type=MESH
        )
    for step in range(1, 8):
        pl.semaphore_signal(
            barrier, inc=1, device_id=(row, lax.rem(col + step, 8)), device_id_type=MESH
        )
    pl.semaphore_wait(barrier, 22)

    def copy(source, landing, send_sems, recv_sems, step, target):
        return pltpu.make_async_remote_copy(
            src_ref=source,
            dst_ref=landing.at[step - 1],
            send_sem=send_sems.at[step - 1],
            recv_sem=recv_sems.at[step - 1],
            device_id=target,
            device_id_type=MESH,
        )

    first = [
        copy(own, by_row, row_send, row_recv, step, (lax.rem(row + step, 16), col))
        for step in range(1, 16)
    ]
    for one in first:
        one.start()
    for one in first:
        one.wait_recv()
    total = own[...]
    for step in range(15):
        total = total + by_row[step]
    middle[...] = total
    second = [
        copy(middle, by_col, col_send, col_recv, step, (row, lax.rem(col + step, 8)))
        for step in range(1, 8)
    ]
    for one in second:
        one.start()
    for one in second:
        one.wait_recv()
    for step in range(7):
        total = total + by_col[step]
    out[...] = total
    for one in first + second:
        one.wait_send()


def sum_devices(own):
    vmem = pl.BlockSpec(memory_space=pltpu.VMEM)
    return pl.pallas_call(
        total_kernel,
        out_shape=jax.ShapeDtypeStruct(own.shape, F32),
        in_specs=[vmem],
        out_specs=vmem,
        scratch_shapes=[
            pltpu.VMEM((15, *own.shape), F32),
            pltpu.VMEM(own.shape, F32),
            pltpu.VMEM((7, *own.shape), F32),
            pltpu.SemaphoreType.DMA((15,)),
            pltpu.SemaphoreType.DMA((15,)),
            pltpu.SemaphoreType.DMA((7,)),
            pltpu.SemaphoreType.DMA((7,)),
        ],
        compiler_params=pltpu.CompilerParams(collective_id=2, has_side_effects=True),
    )(own)


def encode(history, qkv_weight, out_weight, pool_weight):
    row_count = history.shape[0]
    widened = history.astype(jnp.float32)
    inverse = lax.rsqrt(jnp.mean(widened * widened, axis=-1, keepdims=True) + 1e-05)
    normed = (widened * inverse).astype(jnp.bfloat16).reshape(row_count * S, D)
    packed = jnp.dot(normed, qkv_weight, preferred_element_type=jnp.float32).astype(jnp.bfloat16)
    packed = packed.reshape(row_count, S, 3, HEADS, HD)
    query_part = packed[:, :, 0]
    key_part = packed[:, :, 1]
    value_part = packed[:, :, 2]
    logits = jnp.einsum(
        "rshd,rthd->rhst", query_part, key_part, preferred_element_type=jnp.float32
    ) / math.sqrt(HD)
    raised = jnp.exp(logits)
    attention = raised / jnp.sum(raised, axis=-1, keepdims=True)
    attention_low = attention.astype(jnp.bfloat16)
    mixture = jnp.einsum(
        "rhst,rthd->rshd", attention_low, value_part, preferred_element_type=jnp.float32
    )
    mixture = mixture.astype(jnp.bfloat16).reshape(row_count * S, D)
    residual = widened.reshape(row_count * S, D) + jnp.dot(
        mixture, out_weight, preferred_element_type=jnp.float32
    )
    residual_low = residual.astype(jnp.bfloat16)
    active = jnp.tanh(jnp.dot(residual_low, pool_weight, preferred_element_type=jnp.float32))
    pooled = (jnp.sum(active.reshape(row_count, S, D), axis=1) / math.sqrt(S)).astype(jnp.bfloat16)
    stored = (
        widened,
        inverse,
        normed,
        query_part,
        key_part,
        value_part,
        attention,
        attention_low,
        mixture,
        residual_low,
        active,
    )
    return (pooled, stored)


def backward(stored, grad_pooled, qkv_weight, out_weight, pool_weight):
    (
        widened,
        inverse,
        normed,
        query_part,
        key_part,
        value_part,
        attention,
        attention_low,
        mixture,
        residual_low,
        active,
    ) = stored
    row_count = grad_pooled.shape[0]
    grad_active = jnp.broadcast_to(
        grad_pooled[:, None, :] / math.sqrt(S), (row_count, S, D)
    ).reshape(row_count * S, D)
    grad_pre = (grad_active * (1.0 - active * active)).astype(jnp.bfloat16)
    grad_residual = jnp.einsum(
        "ne,de->nd", grad_pre, pool_weight, preferred_element_type=jnp.float32
    )
    grad_residual_low = grad_residual.astype(jnp.bfloat16)
    grad_mixture = jnp.einsum(
        "ne,de->nd", grad_residual_low, out_weight, preferred_element_type=jnp.float32
    )
    grad_mixture = grad_mixture.astype(jnp.bfloat16).reshape(row_count, S, HEADS, HD)
    grad_attention = jnp.einsum(
        "rshd,rthd->rhst", grad_mixture, value_part, preferred_element_type=jnp.float32
    )
    grad_values = jnp.einsum(
        "rhst,rshd->rthd", attention_low, grad_mixture, preferred_element_type=jnp.float32
    )
    grad_logits = (
        attention
        * (grad_attention - jnp.sum(attention * grad_attention, axis=-1, keepdims=True))
        / math.sqrt(HD)
    )
    grad_logits = grad_logits.astype(jnp.bfloat16)
    grad_query = jnp.einsum(
        "rhst,rthd->rshd", grad_logits, key_part, preferred_element_type=jnp.float32
    )
    grad_keys = jnp.einsum(
        "rhst,rshd->rthd", grad_logits, query_part, preferred_element_type=jnp.float32
    )
    grad_packed = (
        jnp.stack([grad_query, grad_keys, grad_values], axis=2)
        .astype(jnp.bfloat16)
        .reshape(row_count * S, 3 * D)
    )
    grad_normed = jnp.einsum(
        "ne,de->nd", grad_packed, qkv_weight, preferred_element_type=jnp.float32
    ).reshape(row_count, S, D)
    grad_input = grad_residual.reshape(row_count, S, D) + inverse * grad_normed
    grad_input = grad_input - widened * inverse**3 * jnp.mean(
        grad_normed * widened, axis=-1, keepdims=True
    )
    return (grad_input, grad_pre, grad_residual_low, grad_packed)


def iota(shape, dim):
    return lax.broadcasted_iota(jnp.int32, shape, dim)


def find_slots(facts, own, me):
    lane = iota((DEVICES, 128), 1)
    local = facts - (R_DEV * me).astype(F32)
    hit = (lane < C_DEV * K) & (local >= 0.0) & (local < float(R_DEV))
    hits = hit.astype(F32)
    before = (iota((128, 128), 0) < iota((128, 128), 1)).astype(BF16)
    order = jnp.dot(hits.astype(BF16), before, preferred_element_type=F32)
    case_of = jnp.where(lane < K, 0.0, jnp.where(lane < 2 * K, 1.0, 2.0))
    columns = [[], [], [], [], []]
    for j in range(CAP):
        chosen = jnp.where(hit & (order == float(j)), 1.0, 0.0)
        row = jnp.sum(chosen * local, axis=1, keepdims=True)
        case = jnp.sum(chosen * case_of, axis=1, keepdims=True)
        taken = jnp.sum(chosen, axis=1, keepdims=True)
        bucket = jnp.zeros_like(row)
        weight = jnp.zeros_like(row)
        for c in range(C_DEV):
            is_c = case == float(c)
            bucket = jnp.where(is_c, facts[:, 96 + c : 97 + c], bucket)
            weight = jnp.where(is_c, facts[:, 99 + c : 100 + c], weight)
        for column, values in zip(columns, (row, case, bucket, weight, taken)):
            column.append(values)
    own_case = iota((16, 1), 0).astype(F32)
    for column, values in zip(
        columns, (own[:, 0:1], own_case, own[:, 1:2], own[:, 2:3], own[:, 3:4])
    ):
        column.append(values)
    return [jnp.concatenate(column, axis=0) for column in columns]


def score_members(row, bucket, pooled, table3, head_weight, risk_weight):
    onehot = (iota((MEMBERS, NB), 1).astype(F32) == bucket).astype(BF16)
    times = jnp.dot(
        jnp.concatenate([onehot] * 3, axis=1), table3, preferred_element_type=F32
    )
    picked = jnp.where(
        row == 0.0, pooled[0:1], jnp.where(row == 1.0, pooled[1:2], pooled[2:3])
    )
    hidden = (picked + times).astype(BF16)
    preact = jnp.dot(hidden, head_weight, preferred_element_type=F32)
    gated = jax.nn.sigmoid(preact)
    score = jnp.sum(preact * gated * risk_weight, axis=1, keepdims=True)
    return hidden, preact, gated, jnp.exp(score)


def partial_sums(raised, case, taken, me):
    raised = jnp.where(taken > 0.0, raised, 0.0)
    lane = iota((DEVICES, 128), 1)
    mine = iota((DEVICES, 128), 0) == me
    sums = jnp.zeros((DEVICES, 128), F32)
    for c in range(C_DEV):
        share = jnp.zeros((DEVICES, 1), F32)
        for j in range(CAP):
            at = slice(j * DEVICES, (j + 1) * DEVICES)
            share = share + jnp.where(case[at] == float(c), raised[at], 0.0)
        share = share + jnp.where(mine, raised[SLOTS + c : SLOTS + c + 1], 0.0)
        sums = jnp.where(lane == c, share, sums)
    return sums.T[0:8]


def score_grads(sums, row, case, weight, taken, raised, preact, gated, risk_weight, head_weight, me):
    denominators = jnp.concatenate([sums, jnp.ones((120, 128), F32)], axis=0).T
    own = jnp.sum(
        jnp.where(iota((16, 128), 1) == me, jnp.concatenate([sums, jnp.ones((8, 128), F32)], axis=0), 0.0),
        axis=1,
        keepdims=True,
    )
    below = jnp.concatenate(
        [
            jnp.where(
                case[j * DEVICES : (j + 1) * DEVICES] == 0.0,
                denominators[:, 0:1],
                jnp.where(
                    case[j * DEVICES : (j + 1) * DEVICES] == 1.0,
                    denominators[:, 1:2],
                    denominators[:, 2:3],
                ),
            )
            for j in range(CAP)
        ]
        + [own],
        axis=0,
    )
    is_case = jnp.where(iota((MEMBERS, 1), 0) >= SLOTS, 1.0, 0.0)
    grad_risk = jnp.where(taken > 0.0, weight * (raised / below - is_case), 0.0)
    grad_preact = (grad_risk * risk_weight * gated * (1.0 + preact * (1.0 - gated))).astype(BF16)
    row_of = jnp.where(
        (iota((MEMBERS, 128), 1).astype(F32) == row) & (taken > 0.0), 1.0, 0.0
    ).astype(BF16)
    by_row = lax.dot_general(
        row_of, grad_preact, (((0,), (0,)), ((), ())), preferred_element_type=F32
    )[0:16]
    high = lax.reduce_precision(by_row, 8, 7)
    both = lax.dot_general(
        jnp.concatenate([high, by_row - high], axis=0).astype(BF16),
        head_weight,
        (((1,), (1,)), ((), ())),
        preferred_element_type=F32,
    )
    return grad_preact, both[0:16] + both[16:32]


def body(
    history,
    qkv_weight,
    out_weight,
    pool_weight,
    head_weight,
    risk_weight,
    time_table,
    case_rows,
    control_rows,
    buckets,
    case_weight,
):
    me = lax.axis_index("rows") * 8 + lax.axis_index("cols")
    mine = jnp.concatenate(
        [
            control_rows.reshape(C_DEV * K).astype(F32),
            buckets.astype(F32),
            case_weight,
            jnp.zeros((128 - C_DEV * (K + 2),), F32),
        ]
    )
    facts = lax.all_gather(mine[None], ("rows", "cols"), axis=0, tiled=True)
    own = jnp.stack(
        [case_rows.astype(F32), buckets.astype(F32), case_weight, jnp.ones((C_DEV,), F32)], axis=1
    )
    own = jnp.pad(own, ((0, 16 - C_DEV), (0, 124)))
    row, case, bucket, weight, taken = find_slots(facts, own, me)
    high = lax.reduce_precision(time_table, 8, 7)
    middle = lax.reduce_precision(time_table - high, 8, 7)
    table3 = jnp.concatenate([high, middle, time_table - high - middle], axis=0).astype(BF16)

    pooled, stored = encode(history, qkv_weight, out_weight, pool_weight)
    risk_row = risk_weight[None]
    hidden, preact, gated, raised = score_members(
        row, bucket, pooled.astype(F32), table3, head_weight, risk_row
    )
    sums = sum_devices(partial_sums(raised, case, taken, me))
    grad_preact, grad_pooled = score_grads(
        sums, row, case, weight, taken, raised, preact, gated, risk_row, head_weight, me
    )
    grad_input, grad_pre, grad_residual_low, grad_packed = backward(
        stored, grad_pooled[:R_DEV], qkv_weight, out_weight, pool_weight
    )
    normed, mixture, residual_low = stored[2], stored[8], stored[9]
    shares = weight_grads(
        normed, mixture, residual_low, hidden, grad_packed, grad_residual_low, grad_pre, grad_preact
    )
    return (grad_input, *shares)


def solution(mesh):
    in_specs = (
        P(("rows", "cols"), None, None),
        P(),
        P(),
        P(),
        P(),
        P(),
        P(),
        P(("rows", "cols")),
        P(("rows", "cols"), None),
        P(("rows", "cols")),
        P(("rows", "cols")),
    )
    out_specs = (
        P(("rows", "cols"), None, None),
        P(("rows", "cols"), None),
        P(("rows", "cols"), None),
        P(("rows", "cols"), None),
        P(("rows", "cols"), None),
    )
    return jax.shard_map(body, mesh=mesh, in_specs=in_specs, out_specs=out_specs, check_vma=False)
```

time: 2270 us -> 233 us (0.10)
  waiting for transfers between devices: 2080 us -> 0 us
  Pallas kernels: 0 us -> 70.7 us
  blocking collectives: 0 us -> 33.1 us
  starting transfers between devices: 27.6 us -> 0 us
    reduce_scatter x4 -> x0, waiting for transfers between devices: 2040 us -> none  [the longest x1 641 us: body(): lax.psum_scatter(pool_grad, ('rows', 'cols'), scatter_dimension=0, tiled=...]
    pallas_call x0 -> x2, Pallas kernels: none -> 70.7 us  [the longest x1 56.8 us: weight_grads(): pl.pallas_call(grads_kernel, out_shape=(jax.ShapeDtypeStruct((8, 3 * D),...]
    all_to_all x3 -> x0, waiting for transfers between devices: 34.6 us -> none  [the longest x1 18 us: body(): lax.all_to_all(buffer.reshape(groups, CAP, D).astype(jnp.bfloat16), ('row...]
    all_gather x0 -> x1, blocking collectives: none -> 33.1 us  [body(): facts = lax.all_gather(mine[None], ('rows', 'cols'), axis=0, tiled=True)]
    all_to_all x3 -> x0, starting transfers between devices: 27.2 us -> none  [the longest x1 11.1 us: body(): lax.all_to_all(requests.reshape(groups, CAP), ('rows', 'cols'), split_axi...]
  transfers between devices with their start and end apart: 7 -> 0, of which waited for: 6 -> 0; matrix products, arithmetic and copies ran while one was open for 5% -> 0% of each run, Pallas kernels for 0% -> 0%
where the time goes in v1:
time: 233 us; the launch traced here: 232 us
  Pallas kernels  70.7 us (30%)
  matrix products  56.4 us (24%)
  local copies, waits for them, and re-layouts  48.8 us (21%)
  blocking collectives  33.1 us (14%)
  other arithmetic  21 us (9%)
    pallas_call x1, Pallas kernels, weight_grads(): pl.pallas_call(grads_kernel, out_shape=(jax.ShapeDtypeStruct((8, 3 * D),...  56.8 us
    all_gather x1, blocking collectives, body(): facts = lax.all_gather(mine[None], ('rows', 'cols'), axis=0, tiled=True)  33.1 us
    unnamed x178, local copies, waits for them, and re-layouts  14.1 us
    pallas_call x1, Pallas kernels, sum_devices(): pl.pallas_call(total_kernel, out_shape=jax.ShapeDtypeStruct(own.shape, F3...  13.9 us
    convert_element_type x3, local copies, waits for them, and re-layouts, backward(): grad_packed = jnp.stack([grad_query, grad_keys, grad_values], axis=2).ast...  13.7 us
    dot_general x1, matrix products, backward(): jnp.einsum('rhst,rthd->rshd', grad_logits, key_part, preferred_element_ty...  7.42 us
    dot_general x1, matrix products, backward(): jnp.einsum('rhst,rshd->rthd', grad_logits, query_part, preferred_element_...  7.3 us
    reshape x1, local copies, waits for them, and re-layouts, encode(): packed = packed.reshape(row_count, S, 3, HEADS, HD)  6.73 us

profile of v1, /device:TPU:0, one launch (start us, length us, event | category | flops | bytes accessed | tf_op | source)
XLA Modules:
  0.0 231.9 jit_solution(2578406643984335489)
XLA Ops:
  0.7 0.8 convert_bitcast_fusion.1
  1.5 0.7 convert_element_type.95
  2.3 0.7 maximum_bitcast_fusion
  3.1 33.1 %all-gather.1 = f32[128,1,128]{2,1,0:T(1,128)S(1)} all-gather(f32[1,1,128]{2,1,0:T(1,128)S(1)} %maximum_bitcast_fusion), channel_id=2, replica_groups=mesh['rows'=16,'cols'=8] {'rows','cols'}, dimensions={0}, use_global_device_ids=true | all-gather | bytes 66048 | tf_op jit(solution)/shard_map/all_gather | solution.py:625
  38.5 0.8 select_reduce_fusion.4
  41.1 0.8 broadcast_compare_fusion
  43.3 1.3 multiply_convert_fusion.2
  44.7 6.7 %convolution_convert_fusion = bf16[384,3072]{1,0:T(8,128)(2,1)} fusion(bf16[384,1024]{1,0:T(8,128)(2,1)S(1)} %bitcast.169, bf16[1024,3072]{1,0:T(8,128)(2,1)} %param.12), kind=kOutput, calls=%fused_computation.4 | convolution fusion | flops 2417098752 | bytes 9437184 | tf_op jit(solution)/shard_map/dot_general | solution.py:400
  51.5 6.7 %reshape.536 = bf16[3,128,3,16,64]{4,3,2,1,0:T(8,128)(2,1)} reshape(bf16[384,3072]{1,0:T(8,128)(2,1)} %convolution_convert_fusion) | data formatting | bytes 4718592 | tf_op jit(solution)/shard_map/reshape | solution.py:401
  58.2 4.9 %fusion.84 = (bf16[3,128,1,16,64]{4,3,2,1,0:T(8,128)(2,1)}, bf16[3,128,1,16,64]{4,3,2,1,0:T(8,128)(2,1)}, bf16[3,128,1,16,64]{4,3,2,1,0:T(8,128)(2,1)}) fusion(bf16[3,128,3,16,64]{4,3,2,1,0:T(8,128)(2,1)} %reshape.536), kind=kLoop, calls=%fused_computation.207 | loop fusion | bytes 4718592 | tf_op jit(solution)/shard_map/slice | solution.py:402
  63.1 2.7 %copy.220 = bf16[3,128,1,16,64]{1,4,3,0,2:T(8,128)(2,1)} copy(bf16[3,128,1,16,64]{4,3,2,1,0:T(8,128)(2,1)} %get-tuple-element.38) | data formatting | bytes 1572864
  65.8 2.7 %copy.221 = bf16[3,128,1,16,64]{1,4,3,0,2:T(8,128)(2,1)} copy(bf16[3,128,1,16,64]{4,3,2,1,0:T(8,128)(2,1)} %get-tuple-element.40) | data formatting | bytes 1572864
  68.5 3.8 %fusion.5 = (f32[3,16,128]{2,1,0:T(8,128)S(1)}, f32[3,16,128,128]{2,3,1,0:T(8,128)}) fusion(bf16[3,128,1,16,64]{1,4,3,0,2:T(8,128)(2,1)} %copy.221, bf16[3,128,1,16,64]{1,4,3,0,2:T(8,128)(2,1)} %copy.220), kind=kOutput, calls=%fused_computation.10 | convolution fusion | flops 102230016 | bytes 4743168 | tf_op jit(solution)/shard_map/rshd,rthd->rhst/dot_general | solution.py:405
  72.2 2.7 %copy.219 = bf16[3,128,1,16,64]{1,4,3,0,2:T(8,128)(2,1)} copy(bf16[3,128,1,16,64]{4,3,2,1,0:T(8,128)(2,1)} %get-tuple-element.39) | data formatting | bytes 1572864
  74.9 2.8 %fusion.24 = bf16[3,128,16,64]{1,3,2,0:T(8,128)(2,1)S(1)} fusion(bf16[3,128,1,16,64]{1,4,3,0,2:T(8,128)(2,1)} %copy.219, f32[3,16,128,128]{2,3,1,0:T(8,128)} %get-tuple-element.84, f32[3,16,128]{2,1,0:T(8,128)S(1)} %get-tuple-element.83), kind=kOutput, calls=%fused_computation.33 | convolution fusion | flops 103415808 | bytes 4743168 | tf_op jit(solution)/shard_map/rhst,rthd->rshd/dot_general | solution.py:411
  77.7 0.7 copy.164
  78.8 0.7 copy-done.17
  79.5 1.0 fusion.15.residual_low
  80.6 2.1 convolution_tanh_fusion
  82.7 2.1 reduce_sum.185
  84.8 0.7 fusion.67
  85.8 1.9 add_convert_fusion.hidden
  87.9 2.9 %multiply_reduce_fusion.1 = (f32[528]{0:T(1024)S(1)}, f32[528,1024]{1,0:T(8,128)}) fusion(f32[1024]{0:T(1024)S(1)} %copy-done.52, bf16[528,1024]{1,0:T(8,128)(2,1)S(1)} %add_convert_fusion.hidden, bf16[1024,1024]{1,0:T(8,128)(2,1)S(1)} %copy-done.16), kind=kOutput, calls=%fused_computation.12 | convolution fusion | flops 1110539776 | bytes 5347392 | tf_op jit(solution)/shard_map/dot_general | solution.py:540
  92.1 1.3 select_add_fusion
  93.4 0.7 select_add_fusion.2
  94.1 0.7 select_select_fusion.4.own
  94.8 13.9 %shard_map.146 = f32[8,128]{1,0:T(8,128)} custom-call(f32[8,128]{1,0:T(8,128)} %select_select_fusion.4.own), custom_call_target="tpu_custom_call" | custom-call | tf_op jit(solution)/shard_map/pallas_call | solution.py:377
  108.7 0.7 pad_bitcast_fusion
  109.5 0.8 select_reduce_fusion.8
  110.6 3.4 %multiply_convert_fusion.1.grad_preact = bf16[528,1024]{1,0:T(8,128)(2,1)} fusion(f32[528,1024]{1,0:T(8,128)} %get-tuple-element.86, f32[528]{0:T(1024)S(1)} %get-tuple-element.34, f32[1024]{0:T(1024)S(1)} %copy-done.52), kind=kLoop, calls=%fused_computation.11 | loop fusion | flops 5406720 | bytes 3250240 | tf_op jit(solution)/shard_map/convert_element_type | solution.py:586
  114.0 1.9 reduce-precision_convert_fusion.2
  115.9 2.3 fusion.61
  118.6 2.2 fusion.88
  120.7 0.9 copy-done.11
  121.6 1.9 convolution_convert_fusion.2
  123.5 2.5 %reshape.537 = bf16[3,128,16,64]{3,2,1,0:T(8,128)(2,1)S(1)} reshape(bf16[384,1024]{1,0:T(8,128)(2,1)} %convolution_convert_fusion.2) | data formatting | bytes 1572864 | tf_op jit(solution)/shard_map/reshape | solution.py:463
  126.0 1.8 copy.197
  127.8 3.7 %fusion.40 = f32[3,16,128,128]{2,3,1,0:T(8,128)} fusion(bf16[3,128,16,64]{1,3,2,0:T(8,128)(2,1)} %copy.197, bf16[3,128,1,16,64]{1,4,3,0,2:T(8,128)(2,1)} %copy.219), kind=kOutput, calls=%fused_computation.50 | convolution fusion | flops 100663296 | bytes 4718592 | tf_op jit(solution)/shard_map/rshd,rthd->rhst/dot_general | solution.py:464
  131.6 7.4 %fusion.18 = bf16[3,128,1,16,64]{1,4,3,0,2:T(8,128)(2,1)} fusion(f32[3,16,128,128]{2,3,1,0:T(8,128)} %fusion.40, bf16[3,128,1,16,64]{1,4,3,0,2:T(8,128)(2,1)S(1)} %copy-done.13, f32[3,16,128,128]{2,3,1,0:T(8,128)} %get-tuple-element.84, f32[3,16,128]{2,1,0:T(8,128)S(1)} %copy-done.38), kind=kOutput, calls=%fused_computation.28 | convolution fusion | flops 107747456 | bytes 7888896 | tf_op jit(solution)/shard_map/rhst,rthd->rshd/dot_general | solution.py:476
  139.0 7.3 %fusion.21 = bf16[3,128,1,16,64]{1,4,3,0,2:T(8,128)(2,1)} fusion(f32[3,16,128,128]{2,3,1,0:T(8,128)} %fusion.40, bf16[3,128,1,16,64]{1,4,3,0,2:T(8,128)(2,1)S(1)} %copy-done.12, f32[3,16,128,128]{2,3,1,0:T(8,128)} %get-tuple-element.84, f32[3,16,128]{2,1,0:T(8,128)S(1)} %copy-done.38), kind=kOutput, calls=%fused_computation.29 | convolution fusion | flops 107747456 | bytes 7888896 | tf_op jit(solution)/shard_map/rhst,rshd->rthd/dot_general | solution.py:479
  146.3 3.2 %convolution_bitcast_fusion = bf16[3,128,1,16,64]{1,4,3,0,2:T(8,128)(2,1)S(1)} fusion(bf16[3,128,16,64]{1,3,2,0:T(8,128)(2,1)S(1)} %copy-done.14, f32[3,16,128,128]{2,3,1,0:T(8,128)} %get-tuple-element.84, f32[3,16,128]{2,1,0:T(8,128)S(1)} %copy-done.38), kind=kOutput, calls=%fused_computation.30 | convolution fusion | flops 103022592 | bytes 4743168 | tf_op jit(solution)/shard_map/rhst,rshd->rthd/dot_general | solution.py:467
  149.5 1.7 maximum_convert_fusion
  151.2 6.3 %copy.213 = bf16[3,128,3,16,64]{4,3,2,1,0:T(8,128)(2,1)} copy(bf16[3,128,3,16,64]{1,4,3,0,2:T(8,128)(2,1)} %maximum_convert_fusion) | data formatting | bytes 4718592 | tf_op jit(solution)/shard_map/convert_element_type | solution.py:484
  157.5 6.9 %reshape.535.grad_packed = bf16[384,3072]{1,0:T(8,128)(2,1)} reshape(bf16[3,128,3,16,64]{4,3,2,1,0:T(8,128)(2,1)} %copy.213) | data formatting | bytes 4718592 | tf_op jit(solution)/shard_map/convert_element_type | solution.py:484
  164.8 56.8 %shard_map.147 = (f32[8,3072]{1,0:T(8,128)S(1)}, f32[8,1024]{1,0:T(8,128)S(1)}, f32[8,1024]{1,0:T(8,128)S(1)}, f32[8,1024]{1,0:T(8,128)S(1)}) custom-call(bf16[384,1024]{1,0:T(8,128)(2,1)S(1)} %bitcast.170, bf16[384,1024]{1,0:T(8,128)(2,1)S(1)} %copy.205.mixture, bf16[384,1024]{1,0:T(8,128)(2,1)} %copy-done.15, bf16[528,1024]{1,0:T(8,128)(2,1)} %copy-done.19, ...), custom_call_target="tpu_custom_call" | custom-call | tf_op jit(solution)/shard_map/pallas_call | solution.py:289
  222.7 5.1 %multiply_reduce_fusion.2 = (f32[3,128]{1,0:T(4,128)S(1)}, f32[3,128,1024]{2,1,0:T(8,128)S(1)}) fusion(bf16[3,128,1024]{2,1,0:T(8,128)(2,1)S(1)} %copy-done.5, bf16[3,128,3072]{1,2,0:T(8,128)(2,1)S(1)} %bitcast.181, bf16[1024,3072]{1,0:T(8,128)(2,1)} %param.12), kind=kOutput, calls=%fused_computation.22 | convolution fusion | flops 2417098240 | bytes 11011584 | tf_op jit(solution)/shard_map/ne,de->nd/dot_general | solution.py:487
  227.9 1.6 multiply_subtract_fusion
  229.4 0.6 copy.281
  (241 shorter events, 11.1 us)
Async XLA Ops:
  0.6 79.9 %copy-start = (bf16[1024,1024]{1,0:T(8,128)(2,1)S(1)}, bf16[1024,1024]{1,0:T(8,128)(2,1)}, u32[]{:S(2)}) copy-start(bf16[1024,1024]{1,0:T(8,128)(2,1)} %param.14) | copy-start | bytes 6291460
  0.6 39.8 %copy-start.60 = (f32[3]{0:T(128)S(1)}, f32[3]{0:T(128)}, u32[]{:S(2)}) copy-start(f32[3]{0:T(128)} %param.21) | copy-start | bytes 40
  0.7 39.6 %copy-start.72 = (s32[3]{0:T(128)S(1)}, s32[3]{0:T(128)}, u32[]{:S(2)}) copy-start(s32[3]{0:T(128)} %param.18) | copy-start | bytes 40
  0.7 41.8 %copy-start.3 = (bf16[3,128,1024]{2,1,0:T(8,128)(2,1)S(1)}, bf16[3,128,1024]{2,1,0:T(8,128)(2,1)}, u32[]{:S(2)}) copy-start(bf16[3,128,1024]{2,1,0:T(8,128)(2,1)} %param.11) | copy-start | bytes 2359300
  36.7 14.7 %copy-start.61 = (f32[128]{0:T(128)}, f32[128]{0:T(128)S(1)}, u32[]{:S(2)}) copy-start(f32[128]{0:T(128)S(1)} %get-tuple-element.31) | copy-start | bytes 1540
  36.7 14.6 %copy-start.63 = (f32[128]{0:T(128)}, f32[128]{0:T(128)S(1)}, u32[]{:S(2)}) copy-start(f32[128]{0:T(128)S(1)} %get-tuple-element.22) | copy-start | bytes 1540
  36.7 14.6 %copy-start.65 = (f32[128]{0:T(128)}, f32[128]{0:T(128)S(1)}, u32[]{:S(2)}) copy-start(f32[128]{0:T(128)S(1)} %get-tuple-element.27) | copy-start | bytes 1540
  36.7 14.6 %copy-start.67 = (f32[128]{0:T(128)}, f32[128]{0:T(128)S(1)}, u32[]{:S(2)}) copy-start(f32[128]{0:T(128)S(1)} %get-tuple-element.28) | copy-start | bytes 1540
  37.7 13.6 %copy-start.27 = (pred[128,1]{1,0:T(8,128)(4,1)}, pred[128,1]{1,0:T(8,128)(4,1)S(1)}, u32[]{:S(2)}) copy-start(pred[128,1]{1,0:T(8,128)(4,1)S(1)} %copy.147) | copy-start | bytes 388
  37.9 13.5 %copy-start.23 = (pred[128,1]{1,0:T(8,128)(4,1)}, pred[128,1]{1,0:T(8,128)(4,1)S(1)}, u32[]{:S(2)}) copy-start(pred[128,1]{1,0:T(8,128)(4,1)S(1)} %copy.148) | copy-start | bytes 388
  38.0 13.3 %copy-start.29 = (pred[128,1]{1,0:T(8,128)(4,1)}, pred[128,1]{1,0:T(8,128)(4,1)S(1)}, u32[]{:S(2)}) copy-start(pred[128,1]{1,0:T(8,128)(4,1)S(1)} %copy.149) | copy-start | bytes 388
  38.2 13.2 %copy-start.31 = (pred[128,1]{1,0:T(8,128)(4,1)}, pred[128,1]{1,0:T(8,128)(4,1)S(1)}, u32[]{:S(2)}) copy-start(pred[128,1]{1,0:T(8,128)(4,1)S(1)} %copy.150) | copy-start | bytes 388
  38.4 13.0 %copy-start.25 = (pred[128,1]{1,0:T(8,128)(4,1)}, pred[128,1]{1,0:T(8,128)(4,1)S(1)}, u32[]{:S(2)}) copy-start(pred[128,1]{1,0:T(8,128)(4,1)S(1)} %copy.151) | copy-start | bytes 388
  38.5 12.9 %copy-start.33 = (pred[128,1]{1,0:T(8,128)(4,1)}, pred[128,1]{1,0:T(8,128)(4,1)S(1)}, u32[]{:S(2)}) copy-start(pred[128,1]{1,0:T(8,128)(4,1)S(1)} %copy.152) | copy-start | bytes 388
  39.9 11.5 %copy-start.35 = (pred[128,1]{1,0:T(8,128)(4,1)}, pred[128,1]{1,0:T(8,128)(4,1)S(1)}, u32[]{:S(2)}) copy-start(pred[128,1]{1,0:T(8,128)(4,1)S(1)} %copy.154) | copy-start | bytes 388
  41.0 10.4 %copy-start.53 = (f32[528,1]{0,1:T(1,128)}, f32[528,1]{0,1:T(1,128)S(1)}, u32[]{:S(2)}) copy-start(f32[528,1]{0,1:T(1,128)S(1)} %get-tuple-element.67) | copy-start | bytes 6340
  41.0 10.4 %copy-start.55 = (f32[528,1]{0,1:T(1,128)}, f32[528,1]{0,1:T(1,128)S(1)}, u32[]{:S(2)}) copy-start(f32[528,1]{0,1:T(1,128)S(1)} %get-tuple-element.36) | copy-start | bytes 6340
  43.3 8.1 %copy-start.39 = (f32[3,128]{1,0:T(4,128)}, f32[3,128]{1,0:T(4,128)S(1)}, u32[]{:S(2)}) copy-start(f32[3,128]{1,0:T(4,128)S(1)} %get-tuple-element.65) | copy-start | bytes 4612
  72.2 5.4 %copy-start.37 = (f32[3,16,128]{2,1,0:T(8,128)}, f32[3,16,128]{2,1,0:T(8,128)S(1)}, u32[]{:S(2)}) copy-start(f32[3,16,128]{2,1,0:T(8,128)S(1)} %get-tuple-element.83) | copy-start | bytes 73732
  80.6 5.0 %copy-start.22 = (f32[128,1024]{1,0:T(8,128)S(1)}, f32[128,1024]{1,0:T(8,128)}, u32[]{:S(2)}) copy-start(f32[128,1024]{1,0:T(8,128)} %param.17) | copy-start | bytes 1572868
  87.7 4.2 %copy-start.24 = (pred[128,1]{1,0:T(8,128)(4,1)S(1)}, pred[128,1]{1,0:T(8,128)(4,1)}, u32[]{:S(2)}) copy-start(pred[128,1]{1,0:T(8,128)(4,1)} %copy-done.23) | copy-start | bytes 388
  87.8 4.2 %copy-start.26 = (pred[128,1]{1,0:T(8,128)(4,1)S(1)}, pred[128,1]{1,0:T(8,128)(4,1)}, u32[]{:S(2)}) copy-start(pred[128,1]{1,0:T(8,128)(4,1)} %copy-done.25) | copy-start | bytes 388
  87.8 4.2 %copy-start.36 = (pred[128,1]{1,0:T(8,128)(4,1)S(1)}, pred[128,1]{1,0:T(8,128)(4,1)}, u32[]{:S(2)}) copy-start(pred[128,1]{1,0:T(8,128)(4,1)} %copy-done.35) | copy-start | bytes 388
  87.8 21.6 %copy-start.51 = (f32[128]{0:T(128)S(1)}, f32[128]{0:T(128)}, u32[]{:S(2)}) copy-start(f32[128]{0:T(128)} %copy-done.50) | copy-start | bytes 1540
  87.8 21.6 %copy-start.49 = (f32[128]{0:T(128)S(1)}, f32[128]{0:T(128)}, u32[]{:S(2)}) copy-start(f32[128]{0:T(128)} %copy-done.48) | copy-start | bytes 1540
  87.8 21.7 %copy-start.47 = (f32[128]{0:T(128)S(1)}, f32[128]{0:T(128)}, u32[]{:S(2)}) copy-start(f32[128]{0:T(128)} %copy-done.46) | copy-start | bytes 1540
  87.8 21.7 %copy-start.45 = (f32[128]{0:T(128)S(1)}, f32[128]{0:T(128)}, u32[]{:S(2)}) copy-start(f32[128]{0:T(128)} %copy-done.44) | copy-start | bytes 1540
  87.8 22.5 %copy-start.71 = (f32[128]{0:T(128)S(1)}, f32[128]{0:T(128)}, u32[]{:S(2)}) copy-start(f32[128]{0:T(128)} %get-tuple-element.16) | copy-start | bytes 1540
  87.8 22.5 %copy-start.70 = (f32[128]{0:T(128)S(1)}, f32[128]{0:T(128)}, u32[]{:S(2)}) copy-start(f32[128]{0:T(128)} %get-tuple-element.17) | copy-start | bytes 1540
  87.8 22.6 %copy-start.69 = (f32[128]{0:T(128)S(1)}, f32[128]{0:T(128)}, u32[]{:S(2)}) copy-start(f32[128]{0:T(128)} %get-tuple-element.15) | copy-start | bytes 1540
  87.8 22.6 %copy-start.68 = (f32[128]{0:T(128)S(1)}, f32[128]{0:T(128)}, u32[]{:S(2)}) copy-start(f32[128]{0:T(128)} %copy-done.67) | copy-start | bytes 1540
  87.9 22.6 %copy-start.66 = (f32[128]{0:T(128)S(1)}, f32[128]{0:T(128)}, u32[]{:S(2)}) copy-start(f32[128]{0:T(128)} %copy-done.65) | copy-start | bytes 1540
  87.9 22.6 %copy-start.64 = (f32[128]{0:T(128)S(1)}, f32[128]{0:T(128)}, u32[]{:S(2)}) copy-start(f32[128]{0:T(128)} %copy-done.63) | copy-start | bytes 1540
  87.9 22.6 %copy-start.62 = (f32[128]{0:T(128)S(1)}, f32[128]{0:T(128)}, u32[]{:S(2)}) copy-start(f32[128]{0:T(128)} %copy-done.61) | copy-start | bytes 1540
  87.9 22.6 %copy-start.42 = (f32[3,4]{0,1:T(4,128)S(1)}, f32[3,4]{0,1:T(4,128)}, u32[]{:S(2)}) copy-start(f32[3,4]{0,1:T(4,128)} %copy-done.41) | copy-start | bytes 148
  87.9 22.6 %copy-start.59 = (f32[16,1]{0,1:T(1,128)S(1)}, f32[16,1]{0,1:T(1,128)}, u32[]{:S(2)}) copy-start(f32[16,1]{0,1:T(1,128)} %get-tuple-element.37) | copy-start | bytes 196
  91.2 22.8 %copy-start.54 = (f32[528,1]{0,1:T(1,128)S(1)}, f32[528,1]{0,1:T(1,128)}, u32[]{:S(2)}) copy-start(f32[528,1]{0,1:T(1,128)} %copy-done.53) | copy-start | bytes 6340
  91.2 22.8 %copy-start.58 = (f32[128]{0:T(128)S(1)}, f32[128]{0:T(128)}, u32[]{:S(2)}) copy-start(f32[128]{0:T(128)} %copy-done.57) | copy-start | bytes 1540
  114.0 4.3 %copy-start.9 = (f32[384,1024]{1,0:T(8,128)S(1)}, f32[384,1024]{1,0:T(8,128)}, u32[]{:S(2)}) copy-start(f32[384,1024]{1,0:T(8,128)} %convolution_tanh_fusion) | copy-start | bytes 4718596
  127.8 3.8 %copy-start.38 = (f32[3,16,128]{2,1,0:T(8,128)S(1)}, f32[3,16,128]{2,1,0:T(8,128)}, u32[]{:S(2)}) copy-start(f32[3,16,128]{2,1,0:T(8,128)} %copy-done.37) | copy-start | bytes 73732
  131.6 7.4 %copy-start.12 = (bf16[3,128,1,16,64]{1,4,3,0,2:T(8,128)(2,1)S(1)}, bf16[3,128,1,16,64]{1,4,3,0,2:T(8,128)(2,1)}, u32[]{:S(2)}) copy-start(bf16[3,128,1,16,64]{1,4,3,0,2:T(8,128)(2,1)} %copy.220) | copy-start | bytes 2359300
  139.0 7.3 %copy-start.14 = (bf16[3,128,16,64]{1,3,2,0:T(8,128)(2,1)S(1)}, bf16[3,128,16,64]{1,3,2,0:T(8,128)(2,1)}, u32[]{:S(2)}) copy-start(bf16[3,128,16,64]{1,3,2,0:T(8,128)(2,1)} %copy.197) | copy-start | bytes 2359300
  157.5 6.9 %copy-start.8 = (bf16[128,8,3,128]{3,1,2,0:T(8,128)(2,1)S(1)}, bf16[128,8,3,128]{3,1,2,0:T(8,128)(2,1)}, u32[]{:S(2)}) copy-start(bf16[128,8,3,128]{3,1,2,0:T(8,128)(2,1)} %copy-done.7) | copy-start | bytes 2359300
  164.8 56.8 %copy-start.2 = (bf16[3,128,3,16,64]{1,4,3,0,2:T(8,128)(2,1)S(1)}, bf16[3,128,3,16,64]{1,4,3,0,2:T(8,128)(2,1)}, u32[]{:S(2)}) copy-start(bf16[3,128,3,16,64]{1,4,3,0,2:T(8,128)(2,1)} %maximum_convert_fusion) | copy-start | bytes 7077892
  222.7 5.2 %copy-start.10 = (f32[384,1024]{1,0:T(8,128)S(1)}, f32[384,1024]{1,0:T(8,128)}, u32[]{:S(2)}) copy-start(f32[384,1024]{1,0:T(8,128)} %get-tuple-element.88) | copy-start | bytes 4718596
  222.7 5.2 %copy-start.40 = (f32[3,128]{1,0:T(4,128)S(1)}, f32[3,128]{1,0:T(4,128)}, u32[]{:S(2)}) copy-start(f32[3,128]{1,0:T(4,128)} %copy-done.39) | copy-start | bytes 4612
  222.7 5.2 %copy-start.43 = (f32[3,128]{1,0:T(4,128)S(1)}, f32[3,128]{1,0:T(4,128)}, u32[]{:S(2)}) copy-start(f32[3,128]{1,0:T(4,128)} %get-tuple-element.64) | copy-start | bytes 4612
  227.8 4.1 %copy-start.1 = (bf16[1024,1024]{1,0:T(8,128)(2,1)S(1)}, bf16[1024,1024]{1,0:T(8,128)(2,1)}, u32[]{:S(2)}) copy-start(bf16[1024,1024]{1,0:T(8,128)(2,1)} %param.14) | copy-start | bytes 6291460
  (25 other events, 58.7 us)

commit v2 on v0

v2 whole, which is shorter than its diff:
```python
import math

import jax
import jax.numpy as jnp
from jax import lax
from jax.experimental import pallas as pl
from jax.experimental.pallas import tpu as pltpu
from jax.sharding import PartitionSpec as P

D = 1024
HD = 64
HEADS = 16
S = 128
K = 32
CAP = 4
NB = 128
R_DEV = 3
C_DEV = 3
TOKENS = R_DEV * S
DEVICES = 128
SLOTS = CAP * DEVICES
MEMBERS = SLOTS + 16
PAIRS = HEADS // 2

MESH = pl.DeviceIdType.MESH
F32 = jnp.float32
BF16 = jnp.bfloat16

WIDE = 512
GROUPS = (
    (0, 0, "zyx"),
    (0, 512, "yxz"),
    (1, 0, "xzy"),
    (1, 512, "zyx"),
    (2, 0, "yxz"),
    (2, 512, "xzy"),
)
COUNT = len(GROUPS)
SPARE = 3


def device_at(place):
    return (place["z"] * 4 + place["y"], place["x"] * 2 + place["core"])


def moved(place, axis, step):
    return {**place, axis: lax.rem(place[axis] + step, 4)}


def remote(source, target, send_sem, recv_sem, device):
    return pltpu.make_async_remote_copy(
        src_ref=source,
        dst_ref=target,
        send_sem=send_sem,
        recv_sem=recv_sem,
        device_id=device,
        device_id_type=MESH,
    )


def added(*parts):
    total = parts[0].astype(F32)
    for part in parts[1:]:
        total = total + part.astype(F32)
    return total


def iota(shape, dim):
    return lax.broadcasted_iota(jnp.int32, shape, dim)


def dot(a, b, contract_a=1, contract_b=0):
    return lax.dot_general(
        a, b, (((contract_a,), (contract_b,)), ((), ())), preferred_element_type=F32
    )


def block(i, size):
    return pl.ds(pl.multiple_of(i * size, size), size)


def loop(count, step, unroll=1):
    def run(i, carry):
        step(i)
        return carry

    lax.fori_loop(0, count, run, 0, unroll=unroll)


def find_slots(facts, own, me):
    lane = iota((DEVICES, 128), 1)
    local = facts - (R_DEV * me).astype(F32)
    hit = (lane < C_DEV * K) & (local >= 0.0) & (local < float(R_DEV))
    hits = jnp.where(hit, 1.0, 0.0)
    before = jnp.where(iota((128, 128), 0) < iota((128, 128), 1), 1.0, 0.0).astype(BF16)
    order = dot(hits.astype(BF16), before)
    case_of = jnp.where(lane < K, 0.0, jnp.where(lane < 2 * K, 1.0, 2.0))
    columns = [[], [], [], [], []]
    for j in range(CAP):
        chosen = jnp.where(order == float(j), hits, 0.0)
        row = jnp.sum(chosen * local, axis=1, keepdims=True)
        case = jnp.sum(chosen * case_of, axis=1, keepdims=True)
        taken = jnp.sum(chosen, axis=1, keepdims=True)
        bucket = jnp.zeros_like(row)
        weight = jnp.zeros_like(row)
        for c in range(C_DEV):
            is_c = case == float(c)
            bucket = jnp.where(is_c, facts[:, 96 + c : 97 + c], bucket)
            weight = jnp.where(is_c, facts[:, 99 + c : 100 + c], weight)
        for column, values in zip(columns, (row, case, bucket, weight, taken)):
            column.append(values)
    own_case = iota((16, 1), 0).astype(F32)
    for column, values in zip(
        columns, (own[:, 0:1], own_case, own[:, 1:2], own[:, 2:3], own[:, 3:4])
    ):
        column.append(values)
    return [jnp.concatenate(column, axis=0) for column in columns]


def partial_sums(raised, case, taken, me):
    raised = jnp.where(taken > 0.0, raised, 0.0)
    lane = iota((DEVICES, 128), 1)
    mine = iota((DEVICES, 128), 0) == me
    sums = jnp.zeros((DEVICES, 128), F32)
    for c in range(C_DEV):
        share = jnp.zeros((DEVICES, 1), F32)
        for j in range(CAP):
            at = slice(j * DEVICES, (j + 1) * DEVICES)
            share = share + jnp.where(case[at] == float(c), raised[at], 0.0)
        share = share + jnp.where(mine, raised[SLOTS + c : SLOTS + c + 1], 0.0)
        sums = jnp.where(lane == c, share, sums)
    return sums.T[0:8]


def risk_grads(sums, case, weight, taken, raised, me):
    denominators = jnp.concatenate([sums, jnp.ones((120, 128), F32)], axis=0).T
    wide = jnp.concatenate([sums, jnp.ones((8, 128), F32)], axis=0)
    own = jnp.sum(jnp.where(iota((16, 128), 1) == me, wide, 0.0), axis=1, keepdims=True)
    below = []
    for j in range(CAP):
        of = case[j * DEVICES : (j + 1) * DEVICES]
        below.append(
            jnp.where(
                of == 0.0,
                denominators[:, 0:1],
                jnp.where(of == 1.0, denominators[:, 1:2], denominators[:, 2:3]),
            )
        )
    below = jnp.concatenate(below + [own], axis=0)
    is_case = jnp.where(iota((MEMBERS, 1), 0) >= SLOTS, 1.0, 0.0)
    return jnp.where(taken > 0.0, weight * (raised / below - is_case), 0.0)


def kernel(
    history_in,
    qkv_in,
    out_in,
    pool_in,
    head_in,
    table_in,
    risk_ref,
    control_ref,
    case_rows,
    buckets,
    case_weight,
    grad_input_out,
    qkv_out,
    out_out,
    pool_out,
    head_out,
    history,
    qkv_weight,
    out_weight,
    pool_weight,
    head_weight,
    table,
    normed,
    inverse,
    packed,
    attention,
    mixture,
    residual_low,
    slope,
    pooled,
    hidden,
    head_slope,
    grad_preact,
    grad_pre,
    grad_residual,
    grad_residual_low,
    grad_mixture,
    grad_packed,
    facts,
    facts_in,
    facts_mine,
    sums_own,
    sums_middle,
    sums_row,
    sums_col,
    part,
    swap,
    first,
    second_sum,
    second,
    third_sum,
    third,
    load_sem,
    store_sem,
    fact_col_send,
    fact_col_recv,
    fact_row_send,
    fact_row_recv,
    sum_row_send,
    sum_row_recv,
    sum_col_send,
    sum_col_recv,
    swap_send,
    swap_recv,
    first_send,
    first_recv,
    second_send,
    second_recv,
    third_send,
    third_recv,
):
    row = lax.axis_index("rows")
    col = lax.axis_index("cols")
    here = {"z": lax.div(row, 4), "y": lax.rem(row, 4), "x": lax.div(col, 2), "core": lax.rem(col, 2)}
    core = here["core"]
    twin = device_at({**here, "core": 1 - core})
    me = row * 8 + col
    row_peers = [(lax.rem(row + step, 16), col) for step in range(1, 16)]
    col_peers = [(row, lax.rem(col + step, 8)) for step in range(1, 8)]
    sends = []

    def send(copy):
        copy.start()
        sends.append(copy)

    def arrived(target, sem):
        remote(target, target, sem, sem, twin).wait_recv()

    loads = [
        pltpu.make_async_copy(source, target, load_sem.at[i])
        for i, (source, target) in enumerate(
            (
                (history_in, history),
                (qkv_in, qkv_weight),
                (table_in, table),
                (out_in, out_weight),
                (pool_in, pool_weight),
                (head_in, head_weight),
            )
        )
    ]
    for copy in loads:
        copy.start()
    barrier = pltpu.get_barrier_semaphore()
    for peer in row_peers + col_peers:
        pl.semaphore_signal(barrier, inc=1, device_id=peer, device_id_type=MESH)
    pl.semaphore_wait(barrier, len(row_peers) + len(col_peers))

    lane = iota((1, 128), 1)
    controls = control_ref[...].astype(F32)
    mine = jnp.concatenate(
        [controls[c : c + 1] for c in range(C_DEV)] + [jnp.zeros((1, 128 - C_DEV * K), F32)], axis=1
    )
    wide_lane, wide_row = iota((16, 128), 1), iota((16, 128), 0)
    own = jnp.where((wide_lane == 3) & (wide_row < C_DEV), 1.0, 0.0)
    for c in range(C_DEV):
        bucket, weight = buckets[c].astype(F32), case_weight[c]
        mine = jnp.where(lane == 96 + c, bucket, mine)
        mine = jnp.where(lane == 99 + c, weight, mine)
        for place, value in enumerate((case_rows[c].astype(F32), bucket, weight)):
            own = jnp.where((wide_lane == place) & (wide_row == c), value, own)
    facts_mine[...] = jnp.broadcast_to(mine, (8, 128))
    for i, peer in enumerate(col_peers):
        send(
            remote(facts_mine, facts_in.at[i], fact_col_send.at[i], fact_col_recv.at[i], peer)
        )

    loads[0].wait()

    def normalise(r):
        rows = block(r, S)
        x = history[rows, :].astype(F32)
        inv = lax.rsqrt(jnp.mean(x * x, axis=1, keepdims=True) + 1e-05)
        inverse[rows, :] = inv
        normed[rows, :] = (x * inv).astype(BF16)

    loop(R_DEV, normalise)
    loads[1].wait()

    def project(n):
        packed[:, block(n, 256)] = dot(normed[...], qkv_weight[:, block(n, 256)]).astype(BF16)

    loop(12, project)

    sub = iota((8, 128), 0)
    tile = jnp.where(sub == col, facts_mine[...], 0.0)
    for i in range(7):
        arrived(facts_in.at[i], fact_col_recv.at[i])
        tile = jnp.where(sub == lax.rem(col + 7 - i, 8), facts_in[i], tile)
    facts[row] = tile
    for i, peer in enumerate(row_peers):
        send(
            remote(facts.at[row], facts.at[row], fact_row_send.at[i], fact_row_recv.at[i], peer)
        )

    low_half = iota((S, 128), 1) < HD

    def halves(values):
        zero = jnp.zeros_like(values)
        return jnp.concatenate(
            [jnp.where(low_half, values, zero), jnp.where(low_half, zero, values)], axis=0
        )

    def joined(values):
        return jnp.where(low_half, values[:S], values[S:])

    def attend_one(r, p):
        rows = block(r, S)
        query = packed[rows, block(p, 128)]
        key = packed[rows, block(PAIRS + p, 128)]
        value = packed[rows, block(2 * PAIRS + p, 128)]
        raised = jnp.exp(dot(query, halves(key), 1, 1) * (1.0 / math.sqrt(HD)))
        low = jnp.concatenate(
            [
                raised[:, :S] / jnp.sum(raised[:, :S], axis=1, keepdims=True),
                raised[:, S:] / jnp.sum(raised[:, S:], axis=1, keepdims=True),
            ],
            axis=1,
        ).astype(BF16)
        attention[r, p] = low
        mixture[rows, block(p, 128)] = dot(low, halves(value)).astype(BF16)

    def attend(i):
        for k in range(4):
            attend_one(lax.div(i, 2), lax.rem(i, 2) * 4 + k)

    loop(2 * R_DEV, attend)
    loads[3].wait()

    def add_residual(n):
        cols = block(n, 256)
        residual = history[:, cols].astype(F32) + dot(mixture[...], out_weight[:, cols])
        residual_low[:, cols] = residual.astype(BF16)

    loop(4, add_residual)
    loads[4].wait()
    sub16 = iota((16, 256), 0)

    def pool(n):
        cols = block(n, 256)
        active = jnp.tanh(dot(residual_low[...], pool_weight[:, cols]))
        slope[:, cols] = (1.0 - active * active) * (1.0 / math.sqrt(S))
        rows = jnp.zeros((16, 256), F32)
        for r in range(R_DEV):
            total = jnp.sum(active[r * S : (r + 1) * S], axis=0, keepdims=True)
            rows = jnp.where(sub16 == r, total * (1.0 / math.sqrt(S)), rows)
        pooled[:, cols] = rows.astype(BF16).astype(F32)

    loop(4, pool)

    for i in range(15):
        source = lax.rem(row + 15 - i, 16)
        arrived(facts.at[source], fact_row_recv.at[i])
    at_row, case, bucket, weight, taken = find_slots(facts[...].reshape(DEVICES, 128), own, me)
    loads[2].wait()
    loads[5].wait()
    onehot = jnp.where(iota((MEMBERS, NB), 1).astype(F32) == bucket, 1.0, 0.0).astype(BF16)
    onehots = jnp.concatenate([onehot] * 3, axis=1)

    def embed(n):
        cols = block(n, 256)
        times = table[:, cols]
        high = times.astype(BF16)
        middle = (times - high.astype(F32)).astype(BF16)
        low = (times - high.astype(F32) - middle.astype(F32)).astype(BF16)
        rows = pooled[:, cols]
        picked = jnp.where(at_row == 0.0, rows[0:1], jnp.where(at_row == 1.0, rows[1:2], rows[2:3]))
        hidden[:, cols] = (
            picked + dot(onehots, jnp.concatenate([high, middle, low], axis=0))
        ).astype(BF16)

    loop(4, embed)

    def score(n, total):
        cols = block(n, 256)
        preact = dot(hidden[...], head_weight[:, cols])
        gated = jax.nn.sigmoid(preact)
        risk = risk_ref[:, cols]
        head_slope[:, cols] = risk * gated * (1.0 + preact * (1.0 - gated))
        return total + jnp.sum(preact * gated * risk, axis=1, keepdims=True)

    raised = jnp.exp(lax.fori_loop(0, 4, score, jnp.zeros((MEMBERS, 1), F32)))

    sums = partial_sums(raised, case, taken, me)
    sums_own[...] = sums
    for i, peer in enumerate(row_peers):
        send(remote(sums_own, sums_row.at[i], sum_row_send.at[i], sum_row_recv.at[i], peer))
    for i in range(15):
        arrived(sums_row.at[i], sum_row_recv.at[i])
        sums = sums + sums_row[i]
    sums_middle[...] = sums
    for i, peer in enumerate(col_peers):
        send(remote(sums_middle, sums_col.at[i], sum_col_send.at[i], sum_col_recv.at[i], peer))
    for i in range(7):
        arrived(sums_col.at[i], sum_col_recv.at[i])
        sums = sums + sums_col[i]

    grad_risk = risk_grads(sums, case, weight, taken, raised, me)
    row_of = jnp.where(
        (iota((MEMBERS, 128), 1).astype(F32) == at_row) & (taken > 0.0), 1.0, 0.0
    ).astype(BF16)

    def score_grad(n):
        cols = block(n, 256)
        grad = (grad_risk * head_slope[:, cols]).astype(BF16)
        grad_preact[:, cols] = grad
        pooled[:, cols] = dot(row_of, grad, 0, 0)[0:16]

    loop(4, score_grad)
    by_row = pooled[...]
    high = by_row.astype(BF16)
    low = (by_row - high.astype(F32)).astype(BF16)
    by_row = jnp.concatenate([high, low], axis=0)

    def pool_grad(n):
        both = dot(by_row, head_weight[block(n, 256), :], 1, 1)
        grad = both[0:16] + both[16:32]
        cols = block(n, 256)
        for r in range(R_DEV):
            rows = slice(r * S, (r + 1) * S)
            grad_pre[rows, cols] = (grad[r : r + 1] * slope[rows, cols]).astype(BF16)

    loop(4, pool_grad)

    slabs = (
        ((residual_low, grad_pre, 0, pool_out, 0), (hidden, grad_preact, 0, head_out, 0)),
        ((mixture, grad_residual_low, 0, out_out, 0), (normed, grad_packed, 2048, qkv_out, 2048)),
        ((normed, grad_packed, 0, qkv_out, 0), (normed, grad_packed, 1024, qkv_out, 1024)),
    )
    swaps = {}

    def produce(g):
        slab, col0, order = GROUPS[g]
        spare = COUNT + g % SPARE
        if g >= SPARE:
            swaps[g - SPARE].wait_send()

        def step(i):
            z = lax.div(i, 2)
            n = lax.rem(i, 2)
            results = [
                dot(lhs[:, block(z, 256)], rhs[:, block((offset + col0) // 256 + n, 256)], 0, 0)
                for lhs, rhs, offset, _, _ in slabs[slab]
            ]
            for y in range(4):
                for x in range(4):
                    for c in range(2):
                        at = y * 64 + x * 16 + c * 8
                        digit = {"z": z, "y": y, "x": x}
                        part[
                            jnp.where(core == c, g, spare),
                            digit[order[0]],
                            digit[order[1]],
                            digit[order[2]],
                            :,
                            block(n, 256),
                        ] = jnp.concatenate([r[at : at + 8] for r in results], axis=0).astype(BF16)

        loop(8, step)
        swaps[g] = remote(part.at[spare], swap.at[g], swap_send.at[g], swap_recv.at[g], twin)
        swaps[g].start()

    def spread(axis, source, landing, send_sems, recv_sems):
        at = here[axis]
        right, left = device_at(moved(here, axis, 1)), device_at(moved(here, axis, 3))
        far = lax.rem(at + 2, 4)
        for slot, digit, half, device in (
            (0, far, 0, right),
            (1, far, 2, left),
            (2, lax.rem(at + 1, 4), 2, right),
            (3, lax.rem(at + 3, 4), 0, left),
        ):
            send(
                remote(
                    source.at[digit, pl.ds(half, 2)],
                    landing.at[slot],
                    send_sems.at[slot],
                    recv_sems.at[slot],
                    device,
                )
            )

    def relay(axis, source, landing, send_sems, recv_sems):
        at = here[axis]
        right, left = device_at(moved(here, axis, 1)), device_at(moved(here, axis, 3))
        for slot, came, digit, half, device in (
            (4, 0, lax.rem(at + 1, 4), 0, right),
            (5, 1, lax.rem(at + 3, 4), 2, left),
        ):
            arrived(landing.at[came], recv_sems.at[came])
            for k in range(2):
                source[digit, half + k] = added(
                    source[digit, half + k], landing[came, k]
                ).astype(BF16)
            send(
                remote(
                    source.at[digit, pl.ds(half, 2)],
                    landing.at[slot],
                    send_sems.at[slot],
                    recv_sems.at[slot],
                    device,
                )
            )

    def collect(axis, source, landing, recv_sems, target):
        at = here[axis]
        for slot in (2, 3, 4, 5):
            arrived(landing.at[slot], recv_sems.at[slot])
        for k in range(2):
            target[k] = added(source[at, k], landing[3, k], landing[4, k]).astype(BF16)
            target[2 + k] = added(source[at, 2 + k], landing[2, k], landing[5, k]).astype(BF16)

    def first_spread(g):
        arrived(swap.at[g], swap_recv.at[g])

        def step(i):
            a, b = lax.div(i, 4), lax.rem(i, 4)
            part[g, a, b] = added(part[g, a, b], swap[g, a, b]).astype(BF16)

        loop(16, step)
        spread(GROUPS[g][2][0], part.at[g], first.at[g], first_send.at[g], first_recv.at[g])

    def first_relay(g):
        relay(GROUPS[g][2][0], part.at[g], first.at[g], first_send.at[g], first_recv.at[g])

    def second_spread(g):
        order = GROUPS[g][2]
        collect(order[0], part.at[g], first.at[g], first_recv.at[g], second_sum.at[g])
        spread(order[1], second_sum.at[g], second.at[g], second_send.at[g], second_recv.at[g])

    def second_relay(g):
        relay(
            GROUPS[g][2][1], second_sum.at[g], second.at[g], second_send.at[g], second_recv.at[g]
        )

    def third_spread(g):
        order = GROUPS[g][2]
        collect(order[1], second_sum.at[g], second.at[g], second_recv.at[g], third_sum.at[g])
        axis = order[2]
        for step in (1, 2, 3):
            send(
                remote(
                    third_sum.at[g, lax.rem(here[axis] + step, 4)],
                    third.at[g, step - 1],
                    third_send.at[g, step - 1],
                    third_recv.at[g, step - 1],
                    device_at(moved(here, axis, step)),
                )
            )

    def finish(g):
        slab, col0, order = GROUPS[g]
        for slot in range(3):
            arrived(third.at[g, slot], third_recv.at[g, slot])
        total = added(third_sum[g, here[order[2]]], third[g, 0], third[g, 1], third[g, 2])
        for t, (_, _, _, out, offset) in enumerate(slabs[slab]):
            out[:, offset + col0 : offset + col0 + WIDE] = total[8 * t : 8 * t + 8]

    def back_residual():
        def step(n):
            cols = block(n, 256)
            grad = dot(grad_pre[...], pool_weight[cols, :], 1, 1)
            grad_residual[:, cols] = grad
            grad_residual_low[:, cols] = grad.astype(BF16)

        loop(4, step)

    def back_mixture():
        def step(n):
            cols = block(n, 256)
            grad_mixture[:, cols] = dot(grad_residual_low[...], out_weight[cols, :], 1, 1).astype(BF16)

        loop(4, step)

    def back_attend_one(r, p):
        rows = block(r, S)
        query = packed[rows, block(p, 128)]
        key = packed[rows, block(PAIRS + p, 128)]
        value = packed[rows, block(2 * PAIRS + p, 128)]
        grad = grad_mixture[rows, block(p, 128)]
        low = attention[r, p]
        weights = low.astype(F32)
        grad_attention = dot(grad, halves(value), 1, 1)
        product = weights * grad_attention
        inner = [
            jnp.sum(product[:, :S], axis=1, keepdims=True),
            jnp.sum(product[:, S:], axis=1, keepdims=True),
        ]
        scale = 1.0 / math.sqrt(HD)
        grad_logits = jnp.concatenate(
            [
                weights[:, :S] * (grad_attention[:, :S] - inner[0]) * scale,
                weights[:, S:] * (grad_attention[:, S:] - inner[1]) * scale,
            ],
            axis=1,
        ).astype(BF16)
        grad_packed[rows, block(p, 128)] = dot(grad_logits, halves(key)).astype(BF16)
        grad_packed[rows, block(PAIRS + p, 128)] = joined(dot(grad_logits, query, 0, 0)).astype(BF16)
        grad_packed[rows, block(2 * PAIRS + p, 128)] = joined(dot(low, grad, 0, 0)).astype(BF16)

    def back_attend(r):
        def step(i):
            for k in range(4):
                back_attend_one(r, i * 4 + k)

        loop(2, step)

    def back_normed(n):
        cols = slice(n * 256, (n + 1) * 256)
        head_slope[0:TOKENS, cols] = dot(grad_packed[...], qkv_weight[cols, :], 1, 1)

    stores = []

    def back_input():
        for r in range(R_DEV):
            rows = slice(r * S, (r + 1) * S)
            grad = head_slope[rows, :]
            x = history[rows, :].astype(F32)
            inv = inverse[rows, :]
            mean = jnp.mean(grad * x, axis=1, keepdims=True)
            head_slope[rows, :] = grad_residual[rows, :] + inv * grad - x * (inv * inv * inv * mean)
            stores.append(
                pltpu.make_async_copy(head_slope.at[rows], grad_input_out.at[rows], store_sem.at[r])
            )
            stores[-1].start()

    a, b, c, d, e, f, g = (
        produce,
        first_spread,
        first_relay,
        second_spread,
        second_relay,
        third_spread,
        finish,
    )
    plan = (
        (a, 0), (a, 1), (back_residual,), (b, 0), (b, 1), (back_mixture,), (c, 0), (c, 1),
        (back_attend, 0), (d, 0), (d, 1), (back_attend, 1), (e, 0), (e, 1), (back_attend, 2),
        (a, 2), (f, 0), (f, 1), (a, 3), (b, 2), (a, 4), (b, 3), (c, 2), (a, 5),
        (b, 4), (c, 3), (d, 2), (g, 0), (g, 1), (back_normed, 0), (b, 5), (c, 4), (d, 3), (e, 2),
        (back_normed, 1), (c, 5), (d, 4), (e, 3), (f, 2), (back_normed, 2), (d, 5), (e, 4), (f, 3),
        (g, 2), (back_normed, 3), (e, 5), (f, 4), (g, 3), (back_input,), (f, 5), (g, 4), (g, 5),
    )
    for stage, *at in plan:
        stage(*at)

    for g in range(COUNT - SPARE, COUNT):
        swaps[g].wait_send()
    for copy in sends:
        copy.wait_send()
    for copy in stores:
        copy.wait()


def body(
    history,
    qkv_weight,
    out_weight,
    pool_weight,
    head_weight,
    risk_weight,
    time_table,
    case_rows,
    control_rows,
    buckets,
    case_weight,
):
    vmem = pl.BlockSpec(memory_space=pltpu.VMEM)
    smem = pl.BlockSpec(memory_space=pltpu.SMEM)
    hbm = pl.BlockSpec(memory_space=pl.ANY)
    dma = pltpu.SemaphoreType.DMA
    grad_input, *shares = pl.pallas_call(
        kernel,
        out_shape=(
            jax.ShapeDtypeStruct((TOKENS, D), F32),
            jax.ShapeDtypeStruct((8, 3 * D), F32),
            jax.ShapeDtypeStruct((8, D), F32),
            jax.ShapeDtypeStruct((8, D), F32),
            jax.ShapeDtypeStruct((8, D), F32),
        ),
        in_specs=[hbm] * 6 + [vmem] * 2 + [smem] * 3,
        out_specs=(hbm,) + (vmem,) * 4,
        scratch_shapes=[
            pltpu.VMEM((TOKENS, D), BF16),
            pltpu.VMEM((D, 3 * D), BF16),
            pltpu.VMEM((D, D), BF16),
            pltpu.VMEM((D, D), BF16),
            pltpu.VMEM((D, D), BF16),
            pltpu.VMEM((NB, D), F32),
            pltpu.VMEM((TOKENS, D), BF16),
            pltpu.VMEM((TOKENS, 1), F32),
            pltpu.VMEM((TOKENS, 3 * D), BF16),
            pltpu.VMEM((R_DEV, PAIRS, S, 2 * S), BF16),
            pltpu.VMEM((TOKENS, D), BF16),
            pltpu.VMEM((TOKENS, D), BF16),
            pltpu.VMEM((TOKENS, D), F32),
            pltpu.VMEM((16, D), F32),
            pltpu.VMEM((MEMBERS, D), BF16),
            pltpu.VMEM((MEMBERS, D), F32),
            pltpu.VMEM((MEMBERS, D), BF16),
            pltpu.VMEM((TOKENS, D), BF16),
            pltpu.VMEM((TOKENS, D), F32),
            pltpu.VMEM((TOKENS, D), BF16),
            pltpu.VMEM((TOKENS, D), BF16),
            pltpu.VMEM((TOKENS, 3 * D), BF16),
            pltpu.VMEM((16, 8, 128), F32),
            pltpu.VMEM((7, 8, 128), F32),
            pltpu.VMEM((8, 128), F32),
            pltpu.VMEM((8, 128), F32),
            pltpu.VMEM((8, 128), F32),
            pltpu.VMEM((15, 8, 128), F32),
            pltpu.VMEM((7, 8, 128), F32),
            pltpu.VMEM((COUNT + SPARE, 4, 4, 4, 16, WIDE), BF16),
            pltpu.VMEM((COUNT, 4, 4, 4, 16, WIDE), BF16),
            pltpu.VMEM((COUNT, 6, 2, 4, 16, WIDE), BF16),
            pltpu.VMEM((COUNT, 4, 4, 16, WIDE), BF16),
            pltpu.VMEM((COUNT, 6, 2, 16, WIDE), BF16),
            pltpu.VMEM((COUNT, 4, 16, WIDE), BF16),
            pltpu.VMEM((COUNT, 3, 16, WIDE), BF16),
            dma((6,)),
            dma((3,)),
            dma((7,)),
            dma((7,)),
            dma((15,)),
            dma((15,)),
            dma((15,)),
            dma((15,)),
            dma((7,)),
            dma((7,)),
            dma((COUNT,)),
            dma((COUNT,)),
            dma((COUNT, 6)),
            dma((COUNT, 6)),
            dma((COUNT, 6)),
            dma((COUNT, 6)),
            dma((COUNT, 3)),
            dma((COUNT, 3)),
        ],
        compiler_params=pltpu.CompilerParams(
            collective_id=1, has_side_effects=True, vmem_limit_bytes=61 * 2**20
        ),
    )(
        history.reshape(TOKENS, D),
        qkv_weight,
        out_weight,
        pool_weight,
        head_weight,
        time_table,
        risk_weight[None],
        control_rows,
        case_rows,
        buckets,
        case_weight,
    )
    return (grad_input.reshape(R_DEV, S, D), *shares)


def solution(mesh):
    in_specs = (
        P(("rows", "cols"), None, None),
        P(),
        P(),
        P(),
        P(),
        P(),
        P(),
        P(("rows", "cols")),
        P(("rows", "cols"), None),
        P(("rows", "cols")),
        P(("rows", "cols")),
    )
    out_specs = (
        P(("rows", "cols"), None, None),
        P(("rows", "cols"), None),
        P(("rows", "cols"), None),
        P(("rows", "cols"), None),
        P(("rows", "cols"), None),
    )
    return jax.shard_map(body, mesh=mesh, in_specs=in_specs, out_specs=out_specs, check_vma=False)
```

time: 2270 us -> 113 us (0.05)
  waiting for transfers between devices: 2080 us -> 0 us
  Pallas kernels: 0 us -> 107 us
  matrix products: 71.3 us -> 0 us
  local copies, waits for them, and re-layouts: 56.7 us -> 5.28 us
  starting transfers between devices: 27.6 us -> 0 us
    reduce_scatter x4 -> x0, waiting for transfers between devices: 2040 us -> none  [the longest x1 641 us: body(): lax.psum_scatter(pool_grad, ('rows', 'cols'), scatter_dimension=0, tiled=...]
    pallas_call x0 -> x1, Pallas kernels: none -> 107 us  [body(): pl.pallas_call(kernel, out_shape=(jax.ShapeDtypeStruct((TOKENS, D), F32),...]
    dot_general x21 -> x0, matrix products: 71.3 us -> none  [the longest x1 7.39 us: backward(): jnp.einsum('rhst,rthd->rshd', grad_logits, key_part, preferred_element_ty...]
    all_to_all x3 -> x0, waiting for transfers between devices: 34.6 us -> none  [the longest x1 18 us: body(): lax.all_to_all(buffer.reshape(groups, CAP, D).astype(jnp.bfloat16), ('row...]
    all_to_all x3 -> x0, starting transfers between devices: 27.2 us -> none  [the longest x1 11.1 us: body(): lax.all_to_all(requests.reshape(groups, CAP), ('rows', 'cols'), split_axi...]
  transfers between devices with their start and end apart: 7 -> 0, of which waited for: 6 -> 0; matrix products, arithmetic and copies ran while one was open for 5% -> 0% of each run, Pallas kernels for 0% -> 0%
where the time goes in v2:
time: 113 us
  Pallas kernels  107 us (95%)
  local copies, waits for them, and re-layouts  5.28 us (5%)
    pallas_call x1, Pallas kernels, body(): pl.pallas_call(kernel, out_shape=(jax.ShapeDtypeStruct((TOKENS, D), F32),...  107 us
    unnamed x13, local copies, waits for them, and re-layouts  5.28 us

profile of v2, /device:TPU:0, one launch (start us, length us, event | category | flops | bytes accessed | tf_op | source)
XLA Modules:
  0.0 113.1 jit_solution(1944749915772005765)
XLA Ops:
  0.6 107.1 %shard_map.146 = (f32[384,1024]{1,0:T(8,128)}, f32[8,3072]{1,0:T(8,128)}, f32[8,1024]{1,0:T(8,128)}, f32[8,1024]{1,0:T(8,128)}, f32[8,1024]{1,0:T(8,128)}) custom-call(bf16[384,1024]{1,0:T(8,128)(2,1)} %bitcast.4, bf16[1024,3072]{1,0:T(8,128)(2,1)} %qkv_in.1, bf16[1024,1024]{1,0:T(8,128)(2,1)} %out_in.1, bf16[1024,1024]{1,0:T(8,128)(2,1)} %pool_in.1, ...), custom_call_target="tpu_custom_call" | custom-call | tf_op jit(solution)/shard_map/pallas_call | solution.py:686
  107.7 0.0 copy-start
  107.8 0.0 copy-start.3
  107.8 0.0 copy-start.2
  107.8 0.0 copy-start.1
  107.8 2.8 %copy.21 = f32[3,128,1024]{2,1,0:T(8,128)} copy(f32[3,128,1024]{2,1,0:T(8,128)} %bitcast.3) | data formatting | bytes 3145728
  110.6 0.0 copy-done
  110.6 0.6 copy.22
  111.2 0.0 copy-done.3
  111.2 0.6 copy.23
  111.8 0.0 copy-done.2
  111.8 0.6 copy.24
  112.4 0.0 copy-done.1
  112.4 0.6 copy.25
Async XLA Ops:
  107.7 2.8 %copy-start = (f32[8,3072]{1,0:T(8,128)S(1)}, f32[8,3072]{1,0:T(8,128)}, u32[]{:S(2)}) copy-start(f32[8,3072]{1,0:T(8,128)} %get-tuple-element.21) | copy-start | bytes 294916
  107.8 3.5 %copy-start.3 = (f32[8,1024]{1,0:T(8,128)S(1)}, f32[8,1024]{1,0:T(8,128)}, u32[]{:S(2)}) copy-start(f32[8,1024]{1,0:T(8,128)} %get-tuple-element.22) | copy-start | bytes 98308
  107.8 4.1 %copy-start.2 = (f32[8,1024]{1,0:T(8,128)S(1)}, f32[8,1024]{1,0:T(8,128)}, u32[]{:S(2)}) copy-start(f32[8,1024]{1,0:T(8,128)} %get-tuple-element.23) | copy-start | bytes 98308
  107.8 4.7 %copy-start.1 = (f32[8,1024]{1,0:T(8,128)S(1)}, f32[8,1024]{1,0:T(8,128)}, u32[]{:S(2)}) copy-start(f32[8,1024]{1,0:T(8,128)} %get-tuple-element.24) | copy-start | bytes 98308

commit v3 on v2

v3 whole, which is shorter than its diff:
```python
import math

import jax
import jax.numpy as jnp
from jax import lax
from jax.experimental import pallas as pl
from jax.experimental.pallas import tpu as pltpu
from jax.sharding import PartitionSpec as P

D = 1024
HD = 64
HEADS = 16
S = 128
K = 32
CAP = 4
NB = 128
R_DEV = 3
C_DEV = 3
TOKENS = R_DEV * S
DEVICES = 128
SLOTS = CAP * DEVICES
MEMBERS = SLOTS + 16
PAIRS = HEADS // 2

MESH = pl.DeviceIdType.MESH
F32 = jnp.float32
BF16 = jnp.bfloat16

GROUPS = (
    (0, 0, 512, "zyx"),
    (0, 512, 256, "yxz"),
    (0, 768, 256, "xzy"),
    (1, 0, 512, "yxz"),
    (2, 0, 512, "xzy"),
    (1, 512, 256, "zyx"),
    (2, 512, 256, "zyx"),
    (1, 768, 256, "yxz"),
    (2, 768, 256, "xzy"),
)
COUNT = len(GROUPS)


def device_at(place):
    return (place["z"] * 4 + place["y"], place["x"] * 2 + place["core"])


def moved(place, axis, step):
    return {**place, axis: lax.rem(place[axis] + step, 4)}


def remote(source, target, send_sem, recv_sem, device):
    return pltpu.make_async_remote_copy(
        src_ref=source,
        dst_ref=target,
        send_sem=send_sem,
        recv_sem=recv_sem,
        device_id=device,
        device_id_type=MESH,
    )


def added(*parts):
    total = parts[0].astype(F32)
    for part in parts[1:]:
        total = total + part.astype(F32)
    return total


def iota(shape, dim):
    return lax.broadcasted_iota(jnp.int32, shape, dim)


def dot(a, b, contract_a=1, contract_b=0):
    return lax.dot_general(
        a, b, (((contract_a,), (contract_b,)), ((), ())), preferred_element_type=F32
    )


def block(i, size):
    return pl.ds(pl.multiple_of(i * size, size), size)


def loop(count, step, unroll=1):
    def run(i, carry):
        step(i)
        return carry

    lax.fori_loop(0, count, run, 0, unroll=unroll)


def find_slots(facts, own, me):
    lane = iota((DEVICES, 128), 1)
    local = facts - (R_DEV * me).astype(F32)
    hit = (lane < C_DEV * K) & (local >= 0.0) & (local < float(R_DEV))
    hits = jnp.where(hit, 1.0, 0.0)
    before = jnp.where(iota((128, 128), 0) < iota((128, 128), 1), 1.0, 0.0).astype(BF16)
    order = dot(hits.astype(BF16), before)
    case_of = jnp.where(lane < K, 0.0, jnp.where(lane < 2 * K, 1.0, 2.0))
    columns = [[], [], [], [], []]
    for j in range(CAP):
        chosen = jnp.where(order == float(j), hits, 0.0)
        row = jnp.sum(chosen * local, axis=1, keepdims=True)
        case = jnp.sum(chosen * case_of, axis=1, keepdims=True)
        taken = jnp.sum(chosen, axis=1, keepdims=True)
        bucket = jnp.zeros_like(row)
        weight = jnp.zeros_like(row)
        for c in range(C_DEV):
            is_c = case == float(c)
            bucket = jnp.where(is_c, facts[:, 96 + c : 97 + c], bucket)
            weight = jnp.where(is_c, facts[:, 99 + c : 100 + c], weight)
        for column, values in zip(columns, (row, case, bucket, weight, taken)):
            column.append(values)
    own_case = iota((16, 1), 0).astype(F32)
    for column, values in zip(
        columns, (own[:, 0:1], own_case, own[:, 1:2], own[:, 2:3], own[:, 3:4])
    ):
        column.append(values)
    return [jnp.concatenate(column, axis=0) for column in columns]


def partial_sums(raised, case, taken, me):
    raised = jnp.where(taken > 0.0, raised, 0.0)
    lane = iota((DEVICES, 128), 1)
    mine = iota((DEVICES, 128), 0) == me
    sums = jnp.zeros((DEVICES, 128), F32)
    for c in range(C_DEV):
        share = jnp.zeros((DEVICES, 1), F32)
        for j in range(CAP):
            at = slice(j * DEVICES, (j + 1) * DEVICES)
            share = share + jnp.where(case[at] == float(c), raised[at], 0.0)
        share = share + jnp.where(mine, raised[SLOTS + c : SLOTS + c + 1], 0.0)
        sums = jnp.where(lane == c, share, sums)
    return sums.T[0:8]


def risk_grads(sums, case, weight, taken, raised, me):
    denominators = jnp.concatenate([sums, jnp.ones((120, 128), F32)], axis=0).T
    wide = jnp.concatenate([sums, jnp.ones((8, 128), F32)], axis=0)
    own = jnp.sum(jnp.where(iota((16, 128), 1) == me, wide, 0.0), axis=1, keepdims=True)
    below = []
    for j in range(CAP):
        of = case[j * DEVICES : (j + 1) * DEVICES]
        below.append(
            jnp.where(
                of == 0.0,
                denominators[:, 0:1],
                jnp.where(of == 1.0, denominators[:, 1:2], denominators[:, 2:3]),
            )
        )
    below = jnp.concatenate(below + [own], axis=0)
    is_case = jnp.where(iota((MEMBERS, 1), 0) >= SLOTS, 1.0, 0.0)
    return jnp.where(taken > 0.0, weight * (raised / below - is_case), 0.0)


def kernel(
    history_in,
    qkv_in,
    out_in,
    pool_in,
    head_in,
    table_in,
    risk_ref,
    control_ref,
    case_rows,
    buckets,
    case_weight,
    grad_input_out,
    qkv_out,
    out_out,
    pool_out,
    head_out,
    history,
    qkv_weight,
    out_weight,
    pool_weight,
    head_weight,
    table,
    normed,
    inverse,
    packed,
    attention,
    mixture,
    residual_low,
    slope,
    pooled,
    hidden,
    head_slope,
    grad_preact,
    grad_residual,
    grad_packed,
    normed_t,
    mixture_t,
    residual_t,
    facts,
    facts_in,
    facts_mine,
    sums_own,
    sums_middle,
    sums_row,
    sums_col,
    load_sem,
    store_sem,
    fact_col_send,
    fact_col_recv,
    fact_row_send,
    fact_row_recv,
    sum_row_send,
    sum_row_recv,
    sum_col_send,
    sum_col_recv,
    swap_send,
    swap_recv,
    first_send,
    first_recv,
    second_send,
    second_recv,
    third_send,
    third_recv,
    *buffers,
):
    part, swap, first, second_sum, second, third_sum, third = (
        buffers[i * COUNT : (i + 1) * COUNT] for i in range(7)
    )
    grad_pre, grad_residual_low, grad_mixture = residual_low, normed, mixture
    row = lax.axis_index("rows")
    col = lax.axis_index("cols")
    here = {"z": lax.div(row, 4), "y": lax.rem(row, 4), "x": lax.div(col, 2), "core": lax.rem(col, 2)}
    core = here["core"]
    twin = device_at({**here, "core": 1 - core})
    me = row * 8 + col
    row_peers = [(lax.rem(row + step, 16), col) for step in range(1, 16)]
    col_peers = [(row, lax.rem(col + step, 8)) for step in range(1, 8)]
    sends = []

    def send(copy):
        copy.start()
        sends.append(copy)

    def arrived(target, sem):
        remote(target, target, sem, sem, twin).wait_recv()

    loads = [
        pltpu.make_async_copy(source, target, load_sem.at[i])
        for i, (source, target) in enumerate(
            (
                (history_in, history),
                (qkv_in.at[:, 0:D], qkv_weight.at[:, 0:D]),
                (qkv_in.at[:, D : 2 * D], qkv_weight.at[:, D : 2 * D]),
                (qkv_in.at[:, 2 * D : 3 * D], qkv_weight.at[:, 2 * D : 3 * D]),
                (out_in, out_weight),
                (pool_in, pool_weight),
                (head_in, head_weight),
                (table_in, table),
            )
        )
    ]
    for copy in loads:
        copy.start()
    barrier = pltpu.get_barrier_semaphore()
    for peer in row_peers + col_peers:
        pl.semaphore_signal(barrier, inc=1, device_id=peer, device_id_type=MESH)
    lane = iota((1, 128), 1)
    controls = control_ref[...].astype(F32)
    mine = jnp.concatenate(
        [controls[c : c + 1] for c in range(C_DEV)] + [jnp.zeros((1, 128 - C_DEV * K), F32)], axis=1
    )
    wide_lane, wide_row = iota((16, 128), 1), iota((16, 128), 0)
    own = jnp.where((wide_lane == 3) & (wide_row < C_DEV), 1.0, 0.0)
    for c in range(C_DEV):
        bucket, weight = buckets[c].astype(F32), case_weight[c]
        mine = jnp.where(lane == 96 + c, bucket, mine)
        mine = jnp.where(lane == 99 + c, weight, mine)
        for place, value in enumerate((case_rows[c].astype(F32), bucket, weight)):
            own = jnp.where((wide_lane == place) & (wide_row == c), value, own)
    facts_mine[...] = jnp.broadcast_to(mine, (8, 128))

    loads[0].wait()

    def normalise(r):
        rows = block(r, S)
        x = history[rows, :].astype(F32)
        inv = lax.rsqrt(jnp.mean(x * x, axis=1, keepdims=True) + 1e-05)
        inverse[rows, :] = inv
        normed[rows, :] = (x * inv).astype(BF16)

    loop(R_DEV, normalise)
    pl.semaphore_wait(barrier, len(row_peers) + len(col_peers))
    for i, peer in enumerate(col_peers):
        send(
            remote(facts_mine, facts_in.at[i], fact_col_send.at[i], fact_col_recv.at[i], peer)
        )
    for n in range(3):
        loads[1 + n].wait()
        cols = slice(n * D, (n + 1) * D)
        packed[:, cols] = dot(normed[...], qkv_weight[:, cols]).astype(BF16)

    sub = iota((8, 128), 0)
    tile = jnp.where(sub == col, facts_mine[...], 0.0)
    for i in range(7):
        arrived(facts_in.at[i], fact_col_recv.at[i])
        tile = jnp.where(sub == lax.rem(col + 7 - i, 8), facts_in[i], tile)
    facts[row] = tile
    for i, peer in enumerate(row_peers):
        send(
            remote(facts.at[row], facts.at[row], fact_row_send.at[i], fact_row_recv.at[i], peer)
        )

    low_half = iota((S, 128), 1) < HD

    def halves(values):
        zero = jnp.zeros_like(values)
        return jnp.concatenate(
            [jnp.where(low_half, values, zero), jnp.where(low_half, zero, values)], axis=0
        )

    def joined(values):
        return jnp.where(low_half, values[:S], values[S:])

    def attend(r):
        rows = block(r, S)
        for p in range(PAIRS):
            query = packed[rows, p * 128 : p * 128 + 128]
            key = packed[rows, D + p * 128 : D + p * 128 + 128]
            value = packed[rows, 2 * D + p * 128 : 2 * D + p * 128 + 128]
            raised = jnp.exp(dot(halves(key), query, 1, 1) * (1.0 / math.sqrt(HD)))
            low = jnp.concatenate(
                [
                    raised[:S] * (1.0 / jnp.sum(raised[:S], axis=0, keepdims=True)),
                    raised[S:] * (1.0 / jnp.sum(raised[S:], axis=0, keepdims=True)),
                ],
                axis=0,
            ).astype(BF16)
            attention[r, p] = low
            mixture[rows, p * 128 : p * 128 + 128] = dot(low, halves(value), 0, 0).astype(BF16)

    loop(R_DEV, attend)
    loads[4].wait()

    def add_residual(n):
        cols = block(n, 512)
        residual = history[:, cols].astype(F32) + dot(mixture[...], out_weight[:, cols])
        residual_low[:, cols] = residual.astype(BF16)

    loop(2, add_residual)
    loads[5].wait()
    sub16 = iota((16, 512), 0)

    def pool(n):
        cols = block(n, 512)
        active = jnp.tanh(dot(residual_low[...], pool_weight[:, cols]))
        slope[:, cols] = (1.0 - active * active) * (1.0 / math.sqrt(S))
        rows = jnp.zeros((16, 512), F32)
        for r in range(R_DEV):
            total = jnp.sum(active[r * S : (r + 1) * S], axis=0, keepdims=True)
            rows = jnp.where(sub16 == r, total * (1.0 / math.sqrt(S)), rows)
        pooled[:, cols] = rows.astype(BF16).astype(F32)

    loop(2, pool)

    for i in range(15):
        source = lax.rem(row + 15 - i, 16)
        arrived(facts.at[source], fact_row_recv.at[i])
    at_row, case, bucket, weight, taken = find_slots(facts[...].reshape(DEVICES, 128), own, me)
    loads[6].wait()
    loads[7].wait()
    onehot = jnp.where(iota((MEMBERS, NB), 1).astype(F32) == bucket, 1.0, 0.0).astype(BF16)
    onehots = jnp.concatenate([onehot] * 3, axis=1)

    def embed(n):
        cols = block(n, 512)
        times = table[:, cols]
        high = times.astype(BF16)
        middle = (times - high.astype(F32)).astype(BF16)
        low = (times - high.astype(F32) - middle.astype(F32)).astype(BF16)
        rows = pooled[:, cols]
        picked = jnp.where(at_row == 0.0, rows[0:1], jnp.where(at_row == 1.0, rows[1:2], rows[2:3]))
        hidden[:, cols] = (
            picked + dot(onehots, jnp.concatenate([high, middle, low], axis=0))
        ).astype(BF16)

    loop(2, embed)

    def score(n, total):
        cols = block(n, 512)
        preact = dot(hidden[...], head_weight[:, cols])
        gated = jax.nn.sigmoid(preact)
        risk = risk_ref[:, cols]
        head_slope[:, cols] = risk * gated * (1.0 + preact * (1.0 - gated))
        return total + jnp.sum(preact * gated * risk, axis=1, keepdims=True)

    raised = jnp.exp(lax.fori_loop(0, 2, score, jnp.zeros((MEMBERS, 1), F32)))

    sums = partial_sums(raised, case, taken, me)
    sums_own[...] = sums
    for i, peer in enumerate(row_peers):
        send(remote(sums_own, sums_row.at[i], sum_row_send.at[i], sum_row_recv.at[i], peer))
    normed_t[...] = normed[...].T
    mixture_t[...] = mixture[...].T
    for i in range(15):
        arrived(sums_row.at[i], sum_row_recv.at[i])
        sums = sums + sums_row[i]
    sums_middle[...] = sums
    for i, peer in enumerate(col_peers):
        send(remote(sums_middle, sums_col.at[i], sum_col_send.at[i], sum_col_recv.at[i], peer))
    residual_t[...] = residual_low[...].T
    for i in range(7):
        arrived(sums_col.at[i], sum_col_recv.at[i])
        sums = sums + sums_col[i]

    grad_risk = risk_grads(sums, case, weight, taken, raised, me)
    row_of = jnp.where(
        (iota((MEMBERS, 128), 1).astype(F32) == at_row) & (taken > 0.0), 1.0, 0.0
    ).astype(BF16)

    def score_grad(n):
        cols = block(n, 512)
        grad = (grad_risk * head_slope[:, cols]).astype(BF16)
        grad_preact[:, cols] = grad
        pooled[:, cols] = dot(row_of, grad, 0, 0)[0:16]

    loop(2, score_grad)
    by_row = pooled[...]
    high = by_row.astype(BF16)
    low = (by_row - high.astype(F32)).astype(BF16)
    by_row = jnp.concatenate([high, low], axis=0)

    def pool_grad(n):
        both = dot(by_row, head_weight[block(n, 512), :], 1, 1)
        grad = both[0:16] + both[16:32]
        cols = block(n, 512)
        for r in range(R_DEV):
            rows = slice(r * S, (r + 1) * S)
            grad_pre[rows, cols] = (grad[r : r + 1] * slope[rows, cols]).astype(BF16)

    loop(2, pool_grad)

    slabs = (
        ((residual_t, 1, grad_pre, 0, pool_out, 0), (hidden, 0, grad_preact, 0, head_out, 0)),
        (
            (mixture_t, 1, grad_residual_low, 0, out_out, 0),
            (normed_t, 1, grad_packed, 2 * D, qkv_out, 2 * D),
        ),
        ((normed_t, 1, grad_packed, 0, qkv_out, 0), (normed_t, 1, grad_packed, D, qkv_out, D)),
    )

    def produce(g):
        slab, col0, width, order = GROUPS[g]
        results = [
            dot(lhs[...], rhs[:, offset + col0 : offset + col0 + width], contract, 0).reshape(
                4, 4, 4, 2, 8, width
            )
            for lhs, contract, rhs, offset, _, _ in slabs[slab]
        ]
        for c in range(2):
            for z in range(4):
                for y in range(4):
                    values = jnp.concatenate(
                        [result[z, y, :, c] for result in results], axis=1
                    ).astype(BF16)
                    if order == "zyx":
                        part[g][c, z, y] = values
                    elif order == "yxz":
                        part[g][c, y, :, z] = values
                    else:
                        part[g][c, :, z, y] = values
        send(remote(part[g].at[1 - core], swap[g], swap_send.at[g], swap_recv.at[g], twin))

    def ring(g):
        at = here[GROUPS[g][3][0]]
        return at, lax.rem(at + 1, 4), lax.rem(at + 2, 4), lax.rem(at + 3, 4)

    def send_first(g, slot, digit, half, step):
        send(
            remote(
                part[g].at[core, digit, pl.ds(half, 2)],
                first[g].at[slot],
                first_send.at[g, slot],
                first_recv.at[g, slot],
                device_at(moved(here, GROUPS[g][3][0], step)),
            )
        )

    def first_spread(g):
        at, right, far, left = ring(g)
        arrived(swap[g], swap_recv.at[g])
        for b in range(4):
            part[g][core, far, b] = added(part[g][core, far, b], swap[g][far, b]).astype(BF16)
        send_first(g, 0, far, 0, 1)
        send_first(g, 1, far, 2, 3)
        for b in range(2):
            part[g][core, right, 2 + b] = added(
                part[g][core, right, 2 + b], swap[g][right, 2 + b]
            ).astype(BF16)
            part[g][core, left, b] = added(part[g][core, left, b], swap[g][left, b]).astype(BF16)
        send_first(g, 2, right, 2, 1)
        send_first(g, 3, left, 0, 3)

    def first_relay(g):
        at, right, far, left = ring(g)
        for slot, came, digit, half, step in ((4, 0, right, 0, 1), (5, 1, left, 2, 3)):
            arrived(first[g].at[came], first_recv.at[g, came])
            for k in range(2):
                b = half + k
                part[g][core, digit, b] = added(
                    part[g][core, digit, b], swap[g][digit, b], first[g][came, k]
                ).astype(BF16)
            send_first(g, slot, digit, half, step)

    def second_spread(g):
        at = ring(g)[0]
        for slot in (2, 3, 4, 5):
            arrived(first[g].at[slot], first_recv.at[g, slot])
        for b in range(4):
            one, other = (3, 4) if b < 2 else (2, 5)
            second_sum[g][b] = added(
                part[g][core, at, b], swap[g][at, b], first[g][one, b % 2], first[g][other, b % 2]
            ).astype(BF16)
        direct(GROUPS[g][3][1], second_sum[g], second[g], second_send.at[g], second_recv.at[g])

    def direct(axis, source, landing, send_sems, recv_sems):
        for step in (2, 1, 3):
            send(
                remote(
                    source.at[lax.rem(here[axis] + step, 4)],
                    landing.at[step - 1],
                    send_sems.at[step - 1],
                    recv_sems.at[step - 1],
                    device_at(moved(here, axis, step)),
                )
            )

    def third_spread(g):
        at = here[GROUPS[g][3][1]]
        for slot in range(3):
            arrived(second[g].at[slot], second_recv.at[g, slot])
        third_sum[g][...] = added(second_sum[g][at], second[g][0], second[g][1], second[g][2]).astype(
            BF16
        )
        direct(GROUPS[g][3][2], third_sum[g], third[g], third_send.at[g], third_recv.at[g])

    def finish(g):
        slab, col0, width, order = GROUPS[g]
        for slot in range(3):
            arrived(third[g].at[slot], third_recv.at[g, slot])
        total = added(third_sum[g][here[order[2]]], third[g][0], third[g][1], third[g][2])
        for t, (_, _, _, _, out, offset) in enumerate(slabs[slab]):
            out[:, offset + col0 : offset + col0 + width] = total[8 * t : 8 * t + 8]

    def back_residual():
        def step(n):
            cols = block(n, 512)
            grad = dot(grad_pre[...], pool_weight[cols, :], 1, 1)
            grad_residual[:, cols] = grad
            grad_residual_low[:, cols] = grad.astype(BF16)

        loop(2, step)

    def back_mixture():
        def step(n):
            cols = block(n, 512)
            grad_mixture[:, cols] = dot(grad_residual_low[...], out_weight[cols, :], 1, 1).astype(BF16)

        loop(2, step)

    def back_attend_one(r, p):
        rows = slice(r * S, (r + 1) * S)
        query_at, key_at, value_at = (slice(i * D + p * 128, i * D + p * 128 + 128) for i in range(3))
        query, key, value = packed[rows, query_at], packed[rows, key_at], packed[rows, value_at]
        grad = grad_mixture[rows, query_at]
        low = attention[r, p]
        weights = low.astype(F32)
        grad_attention = dot(halves(value), grad, 1, 1)
        product = weights * grad_attention
        scale = 1.0 / math.sqrt(HD)
        grad_logits = jnp.concatenate(
            [
                weights[at]
                * (grad_attention[at] - jnp.sum(product[at], axis=0, keepdims=True))
                * scale
                for at in (slice(0, S), slice(S, 2 * S))
            ],
            axis=0,
        ).astype(BF16)
        grad_packed[rows, query_at] = dot(grad_logits, halves(key), 0, 0).astype(BF16)
        grad_packed[rows, key_at] = joined(dot(grad_logits, query)).astype(BF16)
        grad_packed[rows, value_at] = joined(dot(low, grad)).astype(BF16)

    def back_attend(first_pair, pairs):
        for r in range(R_DEV):
            for p in range(first_pair, first_pair + pairs):
                back_attend_one(r, p)

    def back_normed(n):
        cols = slice(n * 512, (n + 1) * 512)
        head_slope[0:TOKENS, cols] = dot(grad_packed[...], qkv_weight[cols, :], 1, 1)

    stores = []

    def back_input():
        for r in range(R_DEV):
            rows = slice(r * S, (r + 1) * S)
            grad = head_slope[rows, :]
            x = history[rows, :].astype(F32)
            inv = inverse[rows, :]
            mean = jnp.mean(grad * x, axis=1, keepdims=True)
            head_slope[rows, :] = grad_residual[rows, :] + inv * grad - x * (inv * inv * inv * mean)
            stores.append(
                pltpu.make_async_copy(head_slope.at[rows], grad_input_out.at[rows], store_sem.at[r])
            )
            stores[-1].start()

    a, b, c, d, e, f = produce, first_spread, first_relay, second_spread, third_spread, finish
    plan = (
        (a, 1), (a, 2), (a, 0), (back_residual,), (b, 1), (b, 2), (back_mixture,), (b, 0), (back_attend, 0, 4), (a, 3), (a, 4), (c, 1), (c, 2), (c, 0), (back_attend, 4, 2), (b, 3), (b, 4), (a, 5), (a, 6), (back_attend, 6, 2), (b, 5), (b, 6), (a, 7), (a, 8), (d, 1), (d, 2), (d, 0), (c, 3), (c, 4), (b, 7), (b, 8), (c, 5), (c, 6), (back_normed, 0), (d, 3), (d, 4), (c, 7), (c, 8), (e, 1), (e, 2), (e, 0), (back_normed, 1), (d, 5), (d, 6), (e, 3), (e, 4), (d, 7), (d, 8), (back_input,), (e, 5), (e, 6), (f, 1), (f, 2), (f, 0), (e, 7), (e, 8), (f, 3), (f, 4), (f, 5), (f, 6), (f, 7), (f, 8),
    )
    for stage, *at in plan:
        stage(*at)

    for copy in sends:
        copy.wait_send()
    for copy in stores:
        copy.wait()


def deliver(results):
    steps = 4

    def copy_kernel(*refs):
        for source, target in zip(refs[: len(results)], refs[len(results) :]):
            target[...] = source[...]

    specs = [pl.BlockSpec((TOKENS // steps, D), lambda i: (i, 0))]
    for result in results[1:]:
        specs.append(pl.BlockSpec((8, result.shape[1] // steps), lambda i: (0, i)))
    return pl.pallas_call(
        copy_kernel,
        grid=(steps,),
        out_shape=tuple(jax.ShapeDtypeStruct(x.shape, x.dtype) for x in results),
        in_specs=specs,
        out_specs=tuple(specs),
    )(*results)


def body(
    history,
    qkv_weight,
    out_weight,
    pool_weight,
    head_weight,
    risk_weight,
    time_table,
    case_rows,
    control_rows,
    buckets,
    case_weight,
):
    vmem = pl.BlockSpec(memory_space=pltpu.VMEM)
    smem = pl.BlockSpec(memory_space=pltpu.SMEM)
    hbm = pl.BlockSpec(memory_space=pl.ANY)
    dma = pltpu.SemaphoreType.DMA
    results = pl.pallas_call(
        kernel,
        out_shape=(
            jax.ShapeDtypeStruct((TOKENS, D), F32),
            jax.ShapeDtypeStruct((8, 3 * D), F32),
            jax.ShapeDtypeStruct((8, D), F32),
            jax.ShapeDtypeStruct((8, D), F32),
            jax.ShapeDtypeStruct((8, D), F32),
        ),
        in_specs=[hbm] * 6 + [vmem] * 2 + [smem] * 3,
        out_specs=(hbm,) + (vmem,) * 4,
        scratch_shapes=[
            pltpu.VMEM((TOKENS, D), BF16),
            pltpu.VMEM((D, 3 * D), BF16),
            pltpu.VMEM((D, D), BF16),
            pltpu.VMEM((D, D), BF16),
            pltpu.VMEM((D, D), BF16),
            pltpu.VMEM((NB, D), F32),
            pltpu.VMEM((TOKENS, D), BF16),
            pltpu.VMEM((TOKENS, 1), F32),
            pltpu.VMEM((TOKENS, 3 * D), BF16),
            pltpu.VMEM((R_DEV, PAIRS, 2 * S, S), BF16),
            pltpu.VMEM((TOKENS, D), BF16),
            pltpu.VMEM((TOKENS, D), BF16),
            pltpu.VMEM((TOKENS, D), F32),
            pltpu.VMEM((16, D), F32),
            pltpu.VMEM((MEMBERS, D), BF16),
            pltpu.VMEM((MEMBERS, D), F32),
            pltpu.VMEM((MEMBERS, D), BF16),
            pltpu.VMEM((TOKENS, D), F32),
            pltpu.VMEM((TOKENS, 3 * D), BF16),
            pltpu.VMEM((D, TOKENS), BF16),
            pltpu.VMEM((D, TOKENS), BF16),
            pltpu.VMEM((D, TOKENS), BF16),
            pltpu.VMEM((16, 8, 128), F32),
            pltpu.VMEM((7, 8, 128), F32),
            pltpu.VMEM((8, 128), F32),
            pltpu.VMEM((8, 128), F32),
            pltpu.VMEM((8, 128), F32),
            pltpu.VMEM((15, 8, 128), F32),
            pltpu.VMEM((7, 8, 128), F32),
            dma((8,)),
            dma((3,)),
            dma((7,)),
            dma((7,)),
            dma((15,)),
            dma((15,)),
            dma((15,)),
            dma((15,)),
            dma((7,)),
            dma((7,)),
            dma((COUNT,)),
            dma((COUNT,)),
            dma((COUNT, 6)),
            dma((COUNT, 6)),
            dma((COUNT, 3)),
            dma((COUNT, 3)),
            dma((COUNT, 3)),
            dma((COUNT, 3)),
        ]
        + [
            pltpu.VMEM((*shape, 16, group[2]), BF16)
            for shape in (
                (2, 4, 4, 4),
                (4, 4, 4),
                (6, 2, 4),
                (4, 4),
                (3, 4),
                (4,),
                (3,),
            )
            for group in GROUPS
        ],
        compiler_params=pltpu.CompilerParams(
            collective_id=1, has_side_effects=True, vmem_limit_bytes=62 * 2**20
        ),
    )(
        history.reshape(TOKENS, D),
        qkv_weight,
        out_weight,
        pool_weight,
        head_weight,
        time_table,
        risk_weight[None],
        control_rows,
        case_rows,
        buckets,
        case_weight,
    )
    grad_input, *shares = deliver(results)
    return (grad_input.reshape(R_DEV, S, D), *shares)


def solution(mesh):
    in_specs = (
        P(("rows", "cols"), None, None),
        P(),
        P(),
        P(),
        P(),
        P(),
        P(),
        P(("rows", "cols")),
        P(("rows", "cols"), None),
        P(("rows", "cols")),
        P(("rows", "cols")),
    )
    out_specs = (
        P(("rows", "cols"), None, None),
        P(("rows", "cols"), None),
        P(("rows", "cols"), None),
        P(("rows", "cols"), None),
        P(("rows", "cols"), None),
    )
    return jax.shard_map(body, mesh=mesh, in_specs=in_specs, out_specs=out_specs, check_vma=False)
```

time: 113 us -> 83.1 us (0.74)
  Pallas kernels: 107 us -> 82.1 us
  local copies, waits for them, and re-layouts: 5.28 us -> 0 us
    pallas_call x1, Pallas kernels: 107 us -> 78.4 us  [body(): pl.pallas_call(kernel, out_shape=(jax.ShapeDtypeStruct((TOKENS, D), F32),...]
    unnamed x13 -> x0, local copies, waits for them, and re-layouts: 5.28 us -> none
    pallas_call x0 -> x1, Pallas kernels: none -> 3.69 us  [deliver(): pl.pallas_call(copy_kernel, grid=(steps,), out_shape=tuple((jax.ShapeDtyp...]
where the time goes in v3:
time: 83.1 us; the launch traced here: 82.9 us
  Pallas kernels  82.1 us (99%)
    pallas_call x1, Pallas kernels, body(): pl.pallas_call(kernel, out_shape=(jax.ShapeDtypeStruct((TOKENS, D), F32),...  78.4 us
    pallas_call x1, Pallas kernels, deliver(): pl.pallas_call(copy_kernel, grid=(steps,), out_shape=tuple((jax.ShapeDtyp...  3.69 us

profile of v3, /device:TPU:0, one launch (start us, length us, event | category | flops | bytes accessed | tf_op | source)
XLA Modules:
  0.0 82.9 jit_solution(5741808351464755010)
XLA Ops:
  0.6 78.4 %shard_map.146 = (f32[384,1024]{1,0:T(8,128)}, f32[8,3072]{1,0:T(8,128)}, f32[8,1024]{1,0:T(8,128)}, f32[8,1024]{1,0:T(8,128)}, f32[8,1024]{1,0:T(8,128)}) custom-call(bf16[384,1024]{1,0:T(8,128)(2,1)} %bitcast.3, bf16[1024,3072]{1,0:T(8,128)(2,1)} %qkv_in.1, bf16[1024,1024]{1,0:T(8,128)(2,1)} %out_in.1, bf16[1024,1024]{1,0:T(8,128)(2,1)} %pool_in.1, ...), custom_call_target="tpu_custom_call" | custom-call | tf_op jit(solution)/shard_map/pallas_call | solution.py:661
  79.1 3.7 %shard_map.147 = (f32[384,1024]{1,0:T(8,128)}, f32[8,3072]{1,0:T(8,128)}, f32[8,1024]{1,0:T(8,128)}, f32[8,1024]{1,0:T(8,128)}, f32[8,1024]{1,0:T(8,128)}) custom-call(f32[384,1024]{1,0:T(8,128)} %get-tuple-element.15.refs_0_, f32[8,3072]{1,0:T(8,128)} %get-tuple-element.16.refs_1_, f32[8,1024]{1,0:T(8,128)} %get-tuple-element.17.refs_2_, ...), custom_call_target="tpu_custom_call" | custom-call | tf_op jit(solution)/shard_map/pallas_call | solution.py:635

commit v4 on v3

--- a/solution.py
+++ b/solution.py
@@ -27,15 +27,15 @@
 BF16 = jnp.bfloat16
 
 GROUPS = (
-    (0, 0, 512, "zyx"),
-    (0, 512, 256, "yxz"),
-    (0, 768, 256, "xzy"),
-    (1, 0, 512, "yxz"),
-    (2, 0, 512, "xzy"),
-    (1, 512, 256, "zyx"),
-    (2, 512, 256, "zyx"),
-    (1, 768, 256, "yxz"),
-    (2, 768, 256, "xzy"),
+    (("head", 0), ("head", 512), 512, "zyx"),
+    (("pool", 0), ("pool", 512), 512, "yxz"),
+    (("out", 0), ("out", 512), 512, "xzy"),
+    (("qkv", 0), ("qkv", D), 256, "zyx"),
+    (("qkv", 256), ("qkv", D + 256), 256, "yxz"),
+    (("qkv", 2 * D), ("qkv", 2 * D + 256), 256, "xzy"),
+    (("qkv", 512), ("qkv", D + 512), 256, "zyx"),
+    (("qkv", 768), ("qkv", D + 768), 256, "yxz"),
+    (("qkv", 2 * D + 512), ("qkv", 2 * D + 768), 256, "xzy"),
 )
 COUNT = len(GROUPS)
 
@@ -130,12 +130,12 @@
             share = share + jnp.where(case[at] == float(c), raised[at], 0.0)
         share = share + jnp.where(mine, raised[SLOTS + c : SLOTS + c + 1], 0.0)
         sums = jnp.where(lane == c, share, sums)
-    return sums.T[0:8]
+    return sums.T[0:4]
 
 
 def risk_grads(sums, case, weight, taken, raised, me):
-    denominators = jnp.concatenate([sums, jnp.ones((120, 128), F32)], axis=0).T
-    wide = jnp.concatenate([sums, jnp.ones((8, 128), F32)], axis=0)
+    denominators = jnp.concatenate([sums, jnp.ones((124, 128), F32)], axis=0).T
+    wide = jnp.concatenate([sums, jnp.ones((12, 128), F32)], axis=0)
     own = jnp.sum(jnp.where(iota((16, 128), 1) == me, wide, 0.0), axis=1, keepdims=True)
     below = []
     for j in range(CAP):
@@ -191,6 +191,7 @@
     normed_t,
     mixture_t,
     residual_t,
+    hidden_t,
     facts,
     facts_in,
     facts_mine,
@@ -403,6 +404,7 @@
     for i, peer in enumerate(col_peers):
         send(remote(sums_middle, sums_col.at[i], sum_col_send.at[i], sum_col_recv.at[i], peer))
     residual_t[...] = residual_low[...].T
+    hidden_t[...] = hidden[...].T
     for i in range(7):
         arrived(sums_col.at[i], sum_col_recv.at[i])
         sums = sums + sums_col[i]
@@ -419,38 +421,20 @@
         pooled[:, cols] = dot(row_of, grad, 0, 0)[0:16]
 
     loop(2, score_grad)
-    by_row = pooled[...]
-    high = by_row.astype(BF16)
-    low = (by_row - high.astype(F32)).astype(BF16)
-    by_row = jnp.concatenate([high, low], axis=0)
-
-    def pool_grad(n):
-        both = dot(by_row, head_weight[block(n, 512), :], 1, 1)
-        grad = both[0:16] + both[16:32]
-        cols = block(n, 512)
-        for r in range(R_DEV):
-            rows = slice(r * S, (r + 1) * S)
-            grad_pre[rows, cols] = (grad[r : r + 1] * slope[rows, cols]).astype(BF16)
-
-    loop(2, pool_grad)
-
-    slabs = (
-        ((residual_t, 1, grad_pre, 0, pool_out, 0), (hidden, 0, grad_preact, 0, head_out, 0)),
-        (
-            (mixture_t, 1, grad_residual_low, 0, out_out, 0),
-            (normed_t, 1, grad_packed, 2 * D, qkv_out, 2 * D),
-        ),
-        ((normed_t, 1, grad_packed, 0, qkv_out, 0), (normed_t, 1, grad_packed, D, qkv_out, D)),
-    )
+    sides = {
+        "head": (hidden_t, 1, grad_preact, head_out),
+        "pool": (residual_t, 1, grad_pre, pool_out),
+        "out": (mixture_t, 1, grad_residual_low, out_out),
+        "qkv": (normed_t, 1, grad_packed, qkv_out),
+    }
 
     def produce(g):
-        slab, col0, width, order = GROUPS[g]
-        results = [
-            dot(lhs[...], rhs[:, offset + col0 : offset + col0 + width], contract, 0).reshape(
-                4, 4, 4, 2, 8, width
-            )
-            for lhs, contract, rhs, offset, _, _ in slabs[slab]
-        ]
+        width, order = GROUPS[g][2:]
+        results = []
+        for name, col0 in GROUPS[g][:2]:
+            lhs, contract, rhs, _ = sides[name]
+            grad = dot(lhs[...], rhs[:, col0 : col0 + width], contract, 0)
+            results.append(grad.reshape(4, 4, 4, 2, 8, width))
         for c in range(2):
             for z in range(4):
                 for y in range(4):
@@ -539,12 +523,28 @@
         direct(GROUPS[g][3][2], third_sum[g], third[g], third_send.at[g], third_recv.at[g])
 
     def finish(g):
-        slab, col0, width, order = GROUPS[g]
+        width, order = GROUPS[g][2:]
         for slot in range(3):
             arrived(third[g].at[slot], third_recv.at[g, slot])
         total = added(third_sum[g][here[order[2]]], third[g][0], third[g][1], third[g][2])
-        for t, (_, _, _, _, out, offset) in enumerate(slabs[slab]):
-            out[:, offset + col0 : offset + col0 + width] = total[8 * t : 8 * t + 8]
+        for t, (name, col0) in enumerate(GROUPS[g][:2]):
+            sides[name][3][:, col0 : col0 + width] = total[8 * t : 8 * t + 8]
+
+    def back_pooled():
+        by_row = pooled[...]
+        high = by_row.astype(BF16)
+        low = (by_row - high.astype(F32)).astype(BF16)
+        by_row = jnp.concatenate([high, low], axis=0)
+
+        def pool_grad(n):
+            both = dot(by_row, head_weight[block(n, 512), :], 1, 1)
+            grad = both[0:16] + both[16:32]
+            cols = block(n, 512)
+            for r in range(R_DEV):
+                rows = slice(r * S, (r + 1) * S)
+                grad_pre[rows, cols] = (grad[r : r + 1] * slope[rows, cols]).astype(BF16)
+
+        loop(2, pool_grad)
 
     def back_residual():
         def step(n):
@@ -610,20 +610,29 @@
             stores[-1].start()
 
     a, b, c, d, e, f = produce, first_spread, first_relay, second_spread, third_spread, finish
+    def drain():
+        while sends:
+            sends.pop(0).wait_send()
+
     plan = (
-        (a, 1), (a, 2), (a, 0), (back_residual,), (b, 1), (b, 2), (back_mixture,), (b, 0), (back_attend, 0, 4), (a, 3), (a, 4), (c, 1), (c, 2), (c, 0), (back_attend, 4, 2), (b, 3), (b, 4), (a, 5), (a, 6), (back_attend, 6, 2), (b, 5), (b, 6), (a, 7), (a, 8), (d, 1), (d, 2), (d, 0), (c, 3), (c, 4), (b, 7), (b, 8), (c, 5), (c, 6), (back_normed, 0), (d, 3), (d, 4), (c, 7), (c, 8), (e, 1), (e, 2), (e, 0), (back_normed, 1), (d, 5), (d, 6), (e, 3), (e, 4), (d, 7), (d, 8), (back_input,), (e, 5), (e, 6), (f, 1), (f, 2), (f, 0), (e, 7), (e, 8), (f, 3), (f, 4), (f, 5), (f, 6), (f, 7), (f, 8),
+        (a, 0), (back_pooled,), (a, 1), (back_residual,), (b, 0), (a, 2), (b, 1), (back_mixture,), (b, 2),
+        (back_attend, 0, 4), (a, 3), (a, 4), (a, 5), (c, 0), (c, 1), (c, 2), (b, 3), (b, 4), (b, 5),
+        (back_attend, 4, 4), (a, 6), (a, 7), (a, 8), (d, 0), (d, 1), (c, 3), (c, 4), (b, 6), (b, 7),
+        (b, 8), (c, 5), (d, 2), (e, 0), (e, 1), (c, 6), (c, 7), (c, 8), (back_normed, 0), (d, 3), (d, 4),
+        (d, 5), (e, 2), (d, 6), (d, 7), (d, 8), (back_normed, 1), (e, 3), (e, 4), (e, 5), (e, 6), (e, 7),
+        (e, 8), (back_input,), (f, 0), (f, 1), (f, 2), (drain,), (f, 3), (f, 4), (f, 5), (f, 6), (f, 7),
+        (f, 8),
     )
     for stage, *at in plan:
         stage(*at)
 
-    for copy in sends:
-        copy.wait_send()
+    drain()
     for copy in stores:
         copy.wait()
 
 
 def deliver(results):
-    steps = 4
+    steps = 2
 
     def copy_kernel(*refs):
         for source, target in zip(refs[: len(results)], refs[len(results) :]):
@@ -692,13 +701,14 @@
             pltpu.VMEM((D, TOKENS), BF16),
             pltpu.VMEM((D, TOKENS), BF16),
             pltpu.VMEM((D, TOKENS), BF16),
+            pltpu.VMEM((D, MEMBERS), BF16),
             pltpu.VMEM((16, 8, 128), F32),
             pltpu.VMEM((7, 8, 128), F32),
             pltpu.VMEM((8, 128), F32),
-            pltpu.VMEM((8, 128), F32),
-            pltpu.VMEM((8, 128), F32),
-            pltpu.VMEM((15, 8, 128), F32),
-            pltpu.VMEM((7, 8, 128), F32),
+            pltpu.VMEM((4, 128), F32),
+            pltpu.VMEM((4, 128), F32),
+            pltpu.VMEM((15, 4, 128), F32),
+            pltpu.VMEM((7, 4, 128), F32),
             dma((8,)),
             dma((3,)),
             dma((7,)),

time: 83.1 us -> 79 us (0.951)
  Pallas kernels: 82.1 us -> 78 us
    pallas_call x1, Pallas kernels: 78.4 us -> 75.6 us  [body(): pl.pallas_call(kernel, out_shape=(jax.ShapeDtypeStruct((TOKENS, D), F32),...]
    pallas_call x1, Pallas kernels: 3.69 us -> 2.45 us  [deliver(): pl.pallas_call(copy_kernel, grid=(steps,), out_shape=tuple((jax.ShapeDtyp...]
where the time goes in v4:
time: 79 us; the launch traced here: 78.8 us
  Pallas kernels  78 us (99%)
  between operations  0.8 us (1%)
    pallas_call x1, Pallas kernels, body(): pl.pallas_call(kernel, out_shape=(jax.ShapeDtypeStruct((TOKENS, D), F32),...  75.6 us
    pallas_call x1, Pallas kernels, deliver(): pl.pallas_call(copy_kernel, grid=(steps,), out_shape=tuple((jax.ShapeDtyp...  2.45 us

profile of v4, /device:TPU:0, one launch (start us, length us, event | category | flops | bytes accessed | tf_op | source)
XLA Modules:
  0.0 78.8 jit_solution(15508070355875118705)
XLA Ops:
  0.6 75.6 %shard_map.146 = (f32[384,1024]{1,0:T(8,128)}, f32[8,3072]{1,0:T(8,128)}, f32[8,1024]{1,0:T(8,128)}, f32[8,1024]{1,0:T(8,128)}, f32[8,1024]{1,0:T(8,128)}) custom-call(bf16[384,1024]{1,0:T(8,128)(2,1)} %bitcast.3, bf16[1024,3072]{1,0:T(8,128)(2,1)} %qkv_in.1, bf16[1024,1024]{1,0:T(8,128)(2,1)} %out_in.1, bf16[1024,1024]{1,0:T(8,128)(2,1)} %pool_in.1, ...), custom_call_target="tpu_custom_call" | custom-call | tf_op jit(solution)/shard_map/pallas_call | solution.py:670
  76.2 2.5 %shard_map.147 = (f32[384,1024]{1,0:T(8,128)}, f32[8,3072]{1,0:T(8,128)}, f32[8,1024]{1,0:T(8,128)}, f32[8,1024]{1,0:T(8,128)}, f32[8,1024]{1,0:T(8,128)}) custom-call(f32[384,1024]{1,0:T(8,128)} %get-tuple-element.15.refs_0_, f32[8,3072]{1,0:T(8,128)} %get-tuple-element.16.refs_1_, f32[8,1024]{1,0:T(8,128)} %get-tuple-element.17.refs_2_, ...), custom_call_target="tpu_custom_call" | custom-call | tf_op jit(solution)/shard_map/pallas_call | solution.py:644

commit v5 on v4

--- a/solution.py
+++ b/solution.py
@@ -284,7 +284,7 @@
         inverse[rows, :] = inv
         normed[rows, :] = (x * inv).astype(BF16)
 
-    loop(R_DEV, normalise)
+    loop(R_DEV, normalise, R_DEV)
     pl.semaphore_wait(barrier, len(row_peers) + len(col_peers))
     for i, peer in enumerate(col_peers):
         send(
@@ -334,7 +334,7 @@
             attention[r, p] = low
             mixture[rows, p * 128 : p * 128 + 128] = dot(low, halves(value), 0, 0).astype(BF16)
 
-    loop(R_DEV, attend)
+    loop(R_DEV, attend, R_DEV)
     loads[4].wait()
 
     def add_residual(n):
@@ -342,7 +342,7 @@
         residual = history[:, cols].astype(F32) + dot(mixture[...], out_weight[:, cols])
         residual_low[:, cols] = residual.astype(BF16)
 
-    loop(2, add_residual)
+    loop(2, add_residual, 2)
     loads[5].wait()
     sub16 = iota((16, 512), 0)
 
@@ -356,7 +356,7 @@
             rows = jnp.where(sub16 == r, total * (1.0 / math.sqrt(S)), rows)
         pooled[:, cols] = rows.astype(BF16).astype(F32)
 
-    loop(2, pool)
+    loop(2, pool, 2)
 
     for i in range(15):
         source = lax.rem(row + 15 - i, 16)
@@ -379,7 +379,7 @@
             picked + dot(onehots, jnp.concatenate([high, middle, low], axis=0))
         ).astype(BF16)
 
-    loop(2, embed)
+    loop(2, embed, 2)
 
     def score(n, total):
         cols = block(n, 512)
@@ -389,7 +389,7 @@
         head_slope[:, cols] = risk * gated * (1.0 + preact * (1.0 - gated))
         return total + jnp.sum(preact * gated * risk, axis=1, keepdims=True)
 
-    raised = jnp.exp(lax.fori_loop(0, 2, score, jnp.zeros((MEMBERS, 1), F32)))
+    raised = jnp.exp(lax.fori_loop(0, 2, score, jnp.zeros((MEMBERS, 1), F32), unroll=2))
 
     sums = partial_sums(raised, case, taken, me)
     sums_own[...] = sums
@@ -420,7 +420,7 @@
         grad_preact[:, cols] = grad
         pooled[:, cols] = dot(row_of, grad, 0, 0)[0:16]
 
-    loop(2, score_grad)
+    loop(2, score_grad, 2)
     sides = {
         "head": (hidden_t, 1, grad_preact, head_out),
         "pool": (residual_t, 1, grad_pre, pool_out),
@@ -544,7 +544,7 @@
                 rows = slice(r * S, (r + 1) * S)
                 grad_pre[rows, cols] = (grad[r : r + 1] * slope[rows, cols]).astype(BF16)
 
-        loop(2, pool_grad)
+        loop(2, pool_grad, 2)
 
     def back_residual():
         def step(n):
@@ -553,14 +553,14 @@
             grad_residual[:, cols] = grad
             grad_residual_low[:, cols] = grad.astype(BF16)
 
-        loop(2, step)
+        loop(2, step, 2)
 
     def back_mixture():
         def step(n):
             cols = block(n, 512)
             grad_mixture[:, cols] = dot(grad_residual_low[...], out_weight[cols, :], 1, 1).astype(BF16)
 
-        loop(2, step)
+        loop(2, step, 2)
 
     def back_attend_one(r, p):
         rows = slice(r * S, (r + 1) * S)

time: 79 us -> 75.8 us (0.959)
  Pallas kernels: 78 us -> 74.8 us
    pallas_call x1, Pallas kernels: 75.6 us -> 72.4 us  [body(): pl.pallas_call(kernel, out_shape=(jax.ShapeDtypeStruct((TOKENS, D), F32),...]
where the time goes in v5:
time: 75.8 us; the launch traced here: 75.6 us
  Pallas kernels  74.8 us (99%)
  between operations  0.82 us (1%)
    pallas_call x1, Pallas kernels, body(): pl.pallas_call(kernel, out_shape=(jax.ShapeDtypeStruct((TOKENS, D), F32),...  72.4 us
    pallas_call x1, Pallas kernels, deliver(): pl.pallas_call(copy_kernel, grid=(steps,), out_shape=tuple((jax.ShapeDtyp...  2.45 us

profile of v5, /device:TPU:0, one launch (start us, length us, event | category | flops | bytes accessed | tf_op | source)
XLA Modules:
  0.0 75.6 jit_solution(1362585127950370240)
XLA Ops:
  0.6 72.4 %shard_map.146 = (f32[384,1024]{1,0:T(8,128)}, f32[8,3072]{1,0:T(8,128)}, f32[8,1024]{1,0:T(8,128)}, f32[8,1024]{1,0:T(8,128)}, f32[8,1024]{1,0:T(8,128)}) custom-call(bf16[384,1024]{1,0:T(8,128)(2,1)} %bitcast.3, bf16[1024,3072]{1,0:T(8,128)(2,1)} %qkv_in.1, bf16[1024,1024]{1,0:T(8,128)(2,1)} %out_in.1, bf16[1024,1024]{1,0:T(8,128)(2,1)} %pool_in.1, ...), custom_call_target="tpu_custom_call" | custom-call | tf_op jit(solution)/shard_map/pallas_call | solution.py:670
  73.0 2.5 %shard_map.147 = (f32[384,1024]{1,0:T(8,128)}, f32[8,3072]{1,0:T(8,128)}, f32[8,1024]{1,0:T(8,128)}, f32[8,1024]{1,0:T(8,128)}, f32[8,1024]{1,0:T(8,128)}) custom-call(f32[384,1024]{1,0:T(8,128)} %get-tuple-element.15.refs_0_, f32[8,3072]{1,0:T(8,128)} %get-tuple-element.16.refs_1_, f32[8,1024]{1,0:T(8,128)} %get-tuple-element.17.refs_2_, ...), custom_call_target="tpu_custom_call" | custom-call | tf_op jit(solution)/shard_map/pallas_call | solution.py:644

commit v6 on v5

--- a/solution.py
+++ b/solution.py
@@ -306,6 +306,8 @@
             remote(facts.at[row], facts.at[row], fact_row_send.at[i], fact_row_recv.at[i], peer)
         )
 
+    for copy in loads[4:]:
+        copy.wait()
     low_half = iota((S, 128), 1) < HD
 
     def halves(values):
@@ -335,7 +337,6 @@
             mixture[rows, p * 128 : p * 128 + 128] = dot(low, halves(value), 0, 0).astype(BF16)
 
     loop(R_DEV, attend, R_DEV)
-    loads[4].wait()
 
     def add_residual(n):
         cols = block(n, 512)
@@ -343,7 +344,6 @@
         residual_low[:, cols] = residual.astype(BF16)
 
     loop(2, add_residual, 2)
-    loads[5].wait()
     sub16 = iota((16, 512), 0)
 
     def pool(n):
@@ -362,8 +362,6 @@
         source = lax.rem(row + 15 - i, 16)
         arrived(facts.at[source], fact_row_recv.at[i])
     at_row, case, bucket, weight, taken = find_slots(facts[...].reshape(DEVICES, 128), own, me)
-    loads[6].wait()
-    loads[7].wait()
     onehot = jnp.where(iota((MEMBERS, NB), 1).astype(F32) == bucket, 1.0, 0.0).astype(BF16)
     onehots = jnp.concatenate([onehot] * 3, axis=1)
 

time: 75.8 us -> 75.8 us (level)
  no operation moved by 1% of the time
where the time goes in v6:
time: 75.8 us; the launch traced here: 75.7 us
  Pallas kernels  74.9 us (99%)
  between operations  0.82 us (1%)
    pallas_call x1, Pallas kernels, body(): pl.pallas_call(kernel, out_shape=(jax.ShapeDtypeStruct((TOKENS, D), F32),...  72.4 us
    pallas_call x1, Pallas kernels, deliver(): pl.pallas_call(copy_kernel, grid=(steps,), out_shape=tuple((jax.ShapeDtyp...  2.45 us

profile of v6, /device:TPU:0, one launch (start us, length us, event | category | flops | bytes accessed | tf_op | source)
XLA Modules:
  0.0 75.7 jit_solution(15957133576198209211)
XLA Ops:
  0.6 72.4 %shard_map.146 = (f32[384,1024]{1,0:T(8,128)}, f32[8,3072]{1,0:T(8,128)}, f32[8,1024]{1,0:T(8,128)}, f32[8,1024]{1,0:T(8,128)}, f32[8,1024]{1,0:T(8,128)}) custom-call(bf16[384,1024]{1,0:T(8,128)(2,1)} %bitcast.3, bf16[1024,3072]{1,0:T(8,128)(2,1)} %qkv_in.1, bf16[1024,1024]{1,0:T(8,128)(2,1)} %out_in.1, bf16[1024,1024]{1,0:T(8,128)(2,1)} %pool_in.1, ...), custom_call_target="tpu_custom_call" | custom-call | tf_op jit(solution)/shard_map/pallas_call | solution.py:668
  73.0 2.5 %shard_map.147 = (f32[384,1024]{1,0:T(8,128)}, f32[8,3072]{1,0:T(8,128)}, f32[8,1024]{1,0:T(8,128)}, f32[8,1024]{1,0:T(8,128)}, f32[8,1024]{1,0:T(8,128)}) custom-call(f32[384,1024]{1,0:T(8,128)} %get-tuple-element.15.refs_0_, f32[8,3072]{1,0:T(8,128)} %get-tuple-element.16.refs_1_, f32[8,1024]{1,0:T(8,128)} %get-tuple-element.17.refs_2_, ...), custom_call_target="tpu_custom_call" | custom-call | tf_op jit(solution)/shard_map/pallas_call | solution.py:642
